TPU v7x, 256 devices: a whole 4x4x8 slice. The times are simulated.
256 devices in a mesh: gx: 32 (over x_hi, z, core), gy: 8 (over x_lo, y).
Axes of the slice: x: 4 (x_hi: 2, x_lo: 2; x = x_hi * 2 + x_lo), y: 4, z: 8, core: 2. Of those that a mesh axis runs over, the one named last changes fastest.
Arguments:
- residual: float32 [4, 3, 16, 256, 2048], P(None, None, None, 'gx', 'gy'), may hold values from -6 to 6
- eps_inv: float32 [16, 256, 2048], P(None, 'gx', 'gy'), may hold values from 0.08 to 1
- region_ids: int32 [16, 256, 2048], P(None, 'gx', 'gy'), may hold values from 0 to 7
- source_mask: int32 [16, 256, 2048], P(None, 'gx', 'gy'), may hold values 0 or 1
- pole_a: float32 [8, 2], replicated, may hold values from 1.2 to 1.9602, as said below
- pole_b: float32 [8, 2], replicated, may hold values from -0.98 to -0.8
- pole_c: float32 [8, 2], replicated, may hold values from 0.1 to 0.4
- waveform: float32 [64, 4], replicated, may hold values from -4 to 4
- plan: int32 [4], replicated, may hold values from 0 to 63
Outputs:
- adjoint_e: float32 [4, 3, 16, 256, 2048], P(None, None, None, 'gx', 'gy')
- adjoint_h: float32 [4, 3, 16, 256, 2048], P(None, None, None, 'gx', 'gy')
Inputs may be any that keep to these rules, and one draw needn't show every extreme that they name: For each region and pole, pole_a is at least 1.2 and below 0.99 * (1 - pole_b), so each pole's recurrence is stable.
All inputs are finite; a program needn't handle non-finite values. No bound on the sum of `source_mask` on one device may be relied on, other than what follows from the above.
Results may differ from a plain program's by a relative error of at most 0.00002.
Values sent between devices are 32-bit elements; how exact they have to be, the bound alone decides.
A program may use at most 64 MiB of HBM per device.

v0:
```python
import jax
import jax.numpy as jnp
from jax import lax
from jax.sharding import PartitionSpec as P

STEPS = 4


def from_behind(value, axis, steps):
    count = lax.axis_size(axis)
    initial, last = (max(0, -steps), min(count, count - steps))
    return lax.ppermute(value, axis, [(source, source + steps) for source in range(initial, last)])


def upper_cell(field, axis):
    count = field.shape[axis]
    inner = lax.slice_in_dim(field, 1, count, axis=axis)
    zeros = jnp.zeros_like(lax.slice_in_dim(field, 0, 1, axis=axis))
    return jnp.concatenate([inner, zeros], axis)


def lower_cell(field, axis):
    count = field.shape[axis]
    inner = lax.slice_in_dim(field, 0, count - 1, axis=axis)
    zeros = jnp.zeros_like(lax.slice_in_dim(field, 0, 1, axis=axis))
    return jnp.concatenate([zeros, inner], axis)


def region_lookup(region_ids, table, pole):
    value = jnp.zeros(region_ids.shape, jnp.float32)
    for region in range(table.shape[0]):
        value = jnp.where(region_ids == region, table[region, pole], value)
    return value


def electric_next(elec):
    elec_x, elec_y, elec_z = elec
    x_faces = from_behind((elec_y[:, :, 0:1, :], elec_z[:, :, 0:1, :]), "gx", -1)
    y_faces = from_behind((elec_x[:, :, :, 0:1], elec_z[:, :, :, 0:1]), "gy", -1)
    return (
        jnp.concatenate([elec_y[:, :, 1:, :], x_faces[0]], 2),
        jnp.concatenate([elec_z[:, :, 1:, :], x_faces[1]], 2),
        jnp.concatenate([elec_x[:, :, :, 1:], y_faces[0]], 3),
        jnp.concatenate([elec_z[:, :, :, 1:], y_faces[1]], 3),
    )


def magnetic_prev(magn):
    magn_x, magn_y, magn_z = magn
    last_x = magn_y.shape[2] - 1
    last_y = magn_x.shape[3] - 1
    x_faces = from_behind((magn_y[:, :, last_x:, :], magn_z[:, :, last_x:, :]), "gx", 1)
    y_faces = from_behind((magn_x[:, :, :, last_y:], magn_z[:, :, :, last_y:]), "gy", 1)
    return (
        jnp.concatenate([x_faces[0], magn_y[:, :, :last_x, :]], 2),
        jnp.concatenate([x_faces[1], magn_z[:, :, :last_x, :]], 2),
        jnp.concatenate([y_faces[0], magn_x[:, :, :, :last_y]], 3),
        jnp.concatenate([y_faces[1], magn_z[:, :, :, :last_y]], 3),
    )


def run_steps(
    residual, eps_cells, mask_float, region_ids, tables, waveform, plan, next_fn, prev_fn
):
    stored = [
        [region_lookup(region_ids, table, pole)[None] for table in tables] for pole in range(2)
    ]
    zeros = jnp.zeros(residual[:, 0].shape, jnp.float32)
    elec = [zeros, zeros, zeros]
    magn = [zeros, zeros, zeros]
    state_u = [[zeros, zeros, zeros], [zeros, zeros, zeros]]
    state_v = [[zeros, zeros, zeros], [zeros, zeros, zeros]]
    samples = jnp.arange(waveform.shape[0], dtype=jnp.int32)[:, None]
    for index_step in range(STEPS):
        amplitude = jnp.sum(jnp.where(samples == plan[index_step], waveform, 0.0), 0)
        scaled = amplitude[:, None, None, None]
        elec = [elec[c] + mask_float * residual[:, c] * scaled for c in range(3)]
        elec_x, elec_y, elec_z = elec
        ey_xnext, ez_xnext, ex_ynext, ez_ynext = next_fn(elec)
        curl_x = ez_ynext - elec_z - (upper_cell(elec_y, 1) - elec_y)
        curl_y = upper_cell(elec_x, 1) - elec_x - (ez_xnext - elec_z)
        curl_z = ey_xnext - elec_y - (ex_ynext - elec_x)
        magn = [magn[0] - 0.5 * curl_x, magn[1] - 0.5 * curl_y, magn[2] - 0.5 * curl_z]
        magn_x, magn_y, magn_z = magn
        hy_xprev, hz_xprev, hx_yprev, hz_yprev = prev_fn(magn)
        back_x = magn_z - hz_yprev - (magn_y - lower_cell(magn_y, 1))
        back_y = magn_x - lower_cell(magn_x, 1) - (magn_z - hz_xprev)
        back_z = magn_y - hy_xprev - (magn_x - hx_yprev)
        backs = [back_x, back_y, back_z]
        sectioned = [elec[c] + 0.5 * eps_cells * backs[c] for c in range(3)]
        change = [zeros, zeros, zeros]
        for pole in range(2):
            coef_a, coef_b, coef_c = stored[pole]
            new_u = [
                coef_a * state_u[pole][c] + state_v[pole][c] + coef_c * sectioned[c]
                for c in range(3)
            ]
            state_v[pole] = [coef_b * state_u[pole][c] for c in range(3)]
            change = [change[c] + (new_u[c] - state_u[pole][c]) for c in range(3)]
            state_u[pole] = new_u
        elec = [sectioned[c] - eps_cells * change[c] for c in range(3)]
    return (jnp.stack(elec, 1), jnp.stack(magn, 1))


def local(residual, eps_inv, region_ids, source_mask, pole_a, pole_b, pole_c, waveform, plan):
    tables = (pole_a, pole_b, pole_c)
    mask_float = source_mask.astype(jnp.float32)[None]
    eps_cells = eps_inv[None]
    return run_steps(
        residual,
        eps_cells,
        mask_float,
        region_ids,
        tables,
        waveform,
        plan,
        electric_next,
        magnetic_prev,
    )


def solution(mesh):
    placed = (
        P(None, None, None, "gx", "gy"),
        P(None, "gx", "gy"),
        P(None, "gx", "gy"),
        P(None, "gx", "gy"),
        P(),
        P(),
        P(),
        P(),
        P(),
    )
    return jax.shard_map(
        local,
        mesh=mesh,
        in_specs=placed,
        out_specs=(P(None, None, None, "gx", "gy"), P(None, None, None, "gx", "gy")),
        check_vma=False,
    )
```

profile of v0, /device:TPU:6, one launch (start us, length us, event | category | flops | bytes accessed | tf_op | source)
XLA Modules:
  0.0 202.1 jit_solution(1191114522933178677)
XLA Ops:
  0.6 1.5 fusion.84
  2.1 0.9 convert_element_type.3
  3.0 1.3 iota_compare_fusion
  4.3 1.3 iota_compare_fusion.2
  5.6 0.8 select_reduce_fusion.1
  6.5 1.7 fusion.72
  8.2 8.0 %collective-permute-start.3 = (f32[4,16,1,256]{3,2,1,0:T(1,128)S(1)}, f32[4,16,1,256]{3,2,1,0:T(1,128)S(1)}, u32[]{:S(2)}, u32[]{:S(2)}) collective-permute-start(f32[4,16,1,256]{3,2,1,0:T(1,128)S(1)} %slice.557), channel_id=1, source_target_pairs={{8,0},{16,8},{24,16},{32,24},{40,32},{48,40},{56,48},{64,56},{72,6... | collective-permute-start | bytes 196616 | tf_op jit(solution)/shard_map/ppermute | solution.py:12
  16.3 2.6 %collective-permute-start = (f32[4,16,1,256]{3,2,1,0:T(1,128)S(1)}, f32[4,16,1,256]{3,2,1,0:T(1,128)S(1)}, u32[]{:S(2)}, u32[]{:S(2)}) collective-permute-start(f32[4,16,1,256]{3,2,1,0:T(1,128)S(1)} %slice.550), channel_id=1, source_target_pairs={{8,0},{16,8},{24,16},{32,24},{40,32},{48,40},{56,48},{64,56},{72,6... | collective-permute-start | bytes 196616 | tf_op jit(solution)/shard_map/ppermute | solution.py:12
  18.9 4.3 %collective-permute-start.4 = (f32[4,16,8,1]{3,2,1,0:T(8,128)S(1)}, f32[4,16,8,1]{3,2,1,0:T(8,128)S(1)}, u32[]{:S(2)}, u32[]{:S(2)}) collective-permute-start(f32[4,16,8,1]{3,2,1,0:T(8,128)S(1)} %slice.560), channel_id=1, source_target_pairs={{1,0},{2,1},{3,2},{4,3},{5,4},{6,5},{7,6},{9,8},{10,9},{11,10},{12... | collective-permute-start | bytes 6152 | tf_op jit(solution)/shard_map/ppermute | solution.py:12
  23.2 2.7 %collective-permute-start.1 = (f32[4,16,8,1]{3,2,1,0:T(8,128)S(1)}, f32[4,16,8,1]{3,2,1,0:T(8,128)S(1)}, u32[]{:S(2)}, u32[]{:S(2)}) collective-permute-start(f32[4,16,8,1]{3,2,1,0:T(8,128)S(1)} %slice.552), channel_id=1, source_target_pairs={{1,0},{2,1},{3,2},{4,3},{5,4},{6,5},{7,6},{9,8},{10,9},{11,10},{12... | collective-permute-start | bytes 6152 | tf_op jit(solution)/shard_map/ppermute | solution.py:12
  25.9 0.7 fusion.82
  26.6 0.7 fusion.81
  27.4 0.7 fusion.83
  28.1 5.2 %broadcast_multiply_fusion.1 = (f32[16,8,256]{2,1,0:T(8,128)S(1)}, f32[16,8,256]{2,1,0:T(8,128)S(1)}, pred[16,8,256]{2,1,0:T(8,128)(4,1)S(1)}, pred[16,8,256]{2,...) fusion(f32[]{:T(128)} %bitcast.44, f32[]{:T(128)} %bitcast.43, ...), kind=kLoop, calls=%fused_computation.155 | loop fusion | flops 557056 | bytes 655392 | tf_op jit(solution)/shard_map/mul | solution.py:98
  33.2 5.1 %broadcast_multiply_fusion.2 = (f32[16,8,256]{2,1,0:T(8,128)S(1)}, f32[16,8,256]{2,1,0:T(8,128)S(1)}) fusion(pred[16,8,256]{2,1,0:T(8,128)(4,1)S(1)} %get-tuple-element.23, pred[16,8,256]{2,1,0:T(8,128)(4,1)S(1)} %get-tuple-element.22, pred[16,8,256]{2,1,0:T(8,128)(4,1)S(1)} %get-tuple-element.21, pred[16,8,256]{2,1,0:T(8,128)(4,1)S(1)} %get-tuple-element.20, ...), kind=kLoop, calls=%fused_computation.156 | loop fusion | flops 294912 | bytes 524320 | tf_op jit(solution)/shard_map/mul | solution.py:95
  38.3 5.0 %select_select_fusion.2 = (f32[16,8,256]{2,1,0:T(8,128)S(1)}, f32[16,8,256]{2,1,0:T(8,128)S(1)}) fusion(pred[16,8,256]{2,1,0:T(8,128)(4,1)S(1)} %get-tuple-element.23, pred[16,8,256]{2,1,0:T(8,128)(4,1)S(1)} %get-tuple-element.22, pred[16,8,256]{2,1,0:T(8,128)(4,1)S(1)} %get-tuple-element.21, pred[16,8,256]{2,1,0:T(8,128)(4,1)S(1)} %get-tuple-element.20, ...), kind=kLoop, calls=%fused_computation.150 | loop fusion | flops 294912 | bytes 655392 | tf_op jit(solution)/shard_map/jit(_where)/select_n | solution.py:32
  43.3 5.1 %broadcast_multiply_fusion.3 = (f32[16,8,256]{2,1,0:T(8,128)S(1)}, f32[16,8,256]{2,1,0:T(8,128)S(1)}) fusion(pred[16,8,256]{2,1,0:T(8,128)(4,1)S(1)} %get-tuple-element.23, pred[16,8,256]{2,1,0:T(8,128)(4,1)S(1)} %get-tuple-element.22, pred[16,8,256]{2,1,0:T(8,128)(4,1)S(1)} %get-tuple-element.21, pred[16,8,256]{2,1,0:T(8,128)(4,1)S(1)} %get-tuple-element.20, ...), kind=kLoop, calls=%fused_computation.157 | loop fusion | flops 294912 | bytes 524320 | tf_op jit(solution)/shard_map/mul | solution.py:95
  49.7 1.9 collective-permute-start.9
  51.8 3.3 %collective-permute-start.10 = (f32[4,16,8,1]{3,2,1,0:T(8,128)S(1)}, f32[4,16,8,1]{3,2,1,0:T(8,128)S(1)}, u32[]{:S(2)}, u32[]{:S(2)}) collective-permute-start(f32[4,16,8,1]{3,2,1,0:T(8,128)S(1)} %slice.574), channel_id=1, source_target_pairs={{0,1},{1,2},{2,3},{3,4},{4,5},{5,6},{6,7},{8,9},{9,10},{10,11},{11... | collective-permute-start | bytes 6152 | tf_op jit(solution)/shard_map/ppermute | solution.py:12
  55.1 5.1 %select_select_fusion.4 = f32[16,8,256]{2,1,0:T(8,128)S(1)} fusion(pred[16,8,256]{2,1,0:T(8,128)(4,1)S(1)} %get-tuple-element.23, pred[16,8,256]{2,1,0:T(8,128)(4,1)S(1)} %get-tuple-element.22, pred[16,8,256]{2,1,0:T(8,128)(4,1)S(1)} %get-tuple-element.21, pred[16,8,256]{2,1,0:T(8,128)(4,1)S(1)} %get-tuple-element.20, ...), kind=kLoop, calls=%fused_computation.152 | loop fusion | flops 262144 | bytes 393248 | tf_op jit(solution)/shard_map/jit(_where)/select_n | solution.py:32
  60.5 1.9 collective-permute-start.5
  62.4 1.9 collective-permute-start.2
  64.9 7.3 %collective-permute-start.11 = (f32[4,16,1,256]{3,2,1,0:T(1,128)S(1)}, f32[4,16,1,256]{3,2,1,0:T(1,128)S(1)}, u32[]{:S(2)}, u32[]{:S(2)}) collective-permute-start(f32[4,16,1,256]{3,2,1,0:T(1,128)S(1)} %slice.577), channel_id=1, source_target_pairs={{8,0},{16,8},{24,16},{32,24},{40,32},{48,40},{56,48},{64,56},{72,6... | collective-permute-start | bytes 196616 | tf_op jit(solution)/shard_map/ppermute | solution.py:12
  72.6 2.4 %collective-permute-start.6 = (f32[4,16,1,256]{3,2,1,0:T(1,128)S(1)}, f32[4,16,1,256]{3,2,1,0:T(1,128)S(1)}, u32[]{:S(2)}, u32[]{:S(2)}) collective-permute-start(f32[4,16,1,256]{3,2,1,0:T(1,128)S(1)} %slice.566), channel_id=1, source_target_pairs={{8,0},{16,8},{24,16},{32,24},{40,32},{48,40},{56,48},{64,56},{72,6... | collective-permute-start | bytes 196616 | tf_op jit(solution)/shard_map/ppermute | solution.py:12
  75.5 5.1 %collective-permute-start.7 = (f32[4,16,8,1]{3,2,1,0:T(8,128)S(1)}, f32[4,16,8,1]{3,2,1,0:T(8,128)S(1)}, u32[]{:S(2)}, u32[]{:S(2)}) collective-permute-start(f32[4,16,8,1]{3,2,1,0:T(8,128)S(1)} %slice.568), channel_id=1, source_target_pairs={{1,0},{2,1},{3,2},{4,3},{5,4},{6,5},{7,6},{9,8},{10,9},{11,10},{12... | collective-permute-start | bytes 6152 | tf_op jit(solution)/shard_map/ppermute | solution.py:12
  80.7 2.8 %collective-permute-start.12 = (f32[4,16,8,1]{3,2,1,0:T(8,128)S(1)}, f32[4,16,8,1]{3,2,1,0:T(8,128)S(1)}, u32[]{:S(2)}, u32[]{:S(2)}) collective-permute-start(f32[4,16,8,1]{3,2,1,0:T(8,128)S(1)} %slice.580), channel_id=1, source_target_pairs={{1,0},{2,1},{3,2},{4,3},{5,4},{6,5},{7,6},{9,8},{10,9},{11,10},{12... | collective-permute-start | bytes 6152 | tf_op jit(solution)/shard_map/ppermute | solution.py:12
  84.1 3.3 %collective-permute-done.7 = f32[4,16,8,1]{3,2,1,0:T(8,128)S(1)} collective-permute-done((f32[4,16,8,1]{3,2,1,0:T(8,128)S(1)}, f32[4,16,8,1]{3,2,1,0:T(8,128)S(1)}, u32[]{:S(2)}, u32[]{:S(2)}) %collective-permute-start.7) | collective-permute-done | bytes 2080 | tf_op jit(solution)/shard_map/ppermute | solution.py:12
  87.3 4.7 %collective-permute-done.12 = f32[4,16,8,1]{3,2,1,0:T(8,128)S(1)} collective-permute-done((f32[4,16,8,1]{3,2,1,0:T(8,128)S(1)}, f32[4,16,8,1]{3,2,1,0:T(8,128)S(1)}, u32[]{:S(2)}, u32[]{:S(2)}) %collective-permute-start.12) | collective-permute-done | bytes 2080 | tf_op jit(solution)/shard_map/ppermute | solution.py:12
  92.7 1.9 collective-permute-start.17
  94.8 2.1 %collective-permute-start.18 = (f32[4,16,8,1]{3,2,1,0:T(8,128)S(1)}, f32[4,16,8,1]{3,2,1,0:T(8,128)S(1)}, u32[]{:S(2)}, u32[]{:S(2)}) collective-permute-start(f32[4,16,8,1]{3,2,1,0:T(8,128)S(1)} %slice.594), channel_id=1, source_target_pairs={{0,1},{1,2},{2,3},{3,4},{4,5},{5,6},{6,7},{8,9},{9,10},{10,11},{11... | collective-permute-start | bytes 6152 | tf_op jit(solution)/shard_map/ppermute | solution.py:12
  96.9 5.1 %broadcast_multiply_fusion = (f32[16,8,256]{2,1,0:T(8,128)S(1)}, f32[16,8,256]{2,1,0:T(8,128)S(1)}) fusion(pred[16,8,256]{2,1,0:T(8,128)(4,1)S(1)} %get-tuple-element.23, pred[16,8,256]{2,1,0:T(8,128)(4,1)S(1)} %get-tuple-element.22, pred[16,8,256]{2,1,0:T(8,128)(4,1)S(1)} %get-tuple-element.21, pred[16,8,256]{2,1,0:T(8,128)(4,1)S(1)} %get-tuple-element.20, ...), kind=kLoop, calls=%fused_computation.154 | loop fusion | flops 294912 | bytes 524320 | tf_op jit(solution)/shard_map/mul | solution.py:98
  102.3 1.9 collective-permute-start.13
  104.2 2.2 %collective-permute-start.8 = (f32[4,16,8,1]{3,2,1,0:T(8,128)S(1)}, f32[4,16,8,1]{3,2,1,0:T(8,128)S(1)}, u32[]{:S(2)}, u32[]{:S(2)}) collective-permute-start(f32[4,16,8,1]{3,2,1,0:T(8,128)S(1)} %slice.569), channel_id=1, source_target_pairs={{0,1},{1,2},{2,3},{3,4},{4,5},{5,6},{6,7},{8,9},{9,10},{10,11},{11... | collective-permute-start | bytes 6152 | tf_op jit(solution)/shard_map/ppermute | solution.py:12
  107.6 6.5 %collective-permute-start.19 = (f32[4,16,1,256]{3,2,1,0:T(1,128)S(1)}, f32[4,16,1,256]{3,2,1,0:T(1,128)S(1)}, u32[]{:S(2)}, u32[]{:S(2)}) collective-permute-start(f32[4,16,1,256]{3,2,1,0:T(1,128)S(1)} %slice.597), channel_id=1, source_target_pairs={{8,0},{16,8},{24,16},{32,24},{40,32},{48,40},{56,48},{64,56},{72,6... | collective-permute-start | bytes 196616 | tf_op jit(solution)/shard_map/ppermute | solution.py:12
  114.7 2.4 %collective-permute-start.14 = (f32[4,16,1,256]{3,2,1,0:T(1,128)S(1)}, f32[4,16,1,256]{3,2,1,0:T(1,128)S(1)}, u32[]{:S(2)}, u32[]{:S(2)}) collective-permute-start(f32[4,16,1,256]{3,2,1,0:T(1,128)S(1)} %slice.586), channel_id=1, source_target_pairs={{8,0},{16,8},{24,16},{32,24},{40,32},{48,40},{56,48},{64,56},{72,6... | collective-permute-start | bytes 196616 | tf_op jit(solution)/shard_map/ppermute | solution.py:12
  117.8 6.3 %collective-permute-start.15 = (f32[4,16,8,1]{3,2,1,0:T(8,128)S(1)}, f32[4,16,8,1]{3,2,1,0:T(8,128)S(1)}, u32[]{:S(2)}, u32[]{:S(2)}) collective-permute-start(f32[4,16,8,1]{3,2,1,0:T(8,128)S(1)} %slice.588), channel_id=1, source_target_pairs={{1,0},{2,1},{3,2},{4,3},{5,4},{6,5},{7,6},{9,8},{10,9},{11,10},{12... | collective-permute-start | bytes 6152 | tf_op jit(solution)/shard_map/ppermute | solution.py:12
  124.1 3.9 %collective-permute-start.20 = (f32[4,16,8,1]{3,2,1,0:T(8,128)S(1)}, f32[4,16,8,1]{3,2,1,0:T(8,128)S(1)}, u32[]{:S(2)}, u32[]{:S(2)}) collective-permute-start(f32[4,16,8,1]{3,2,1,0:T(8,128)S(1)} %slice.600), channel_id=1, source_target_pairs={{1,0},{2,1},{3,2},{4,3},{5,4},{6,5},{7,6},{9,8},{10,9},{11,10},{12... | collective-permute-start | bytes 6152 | tf_op jit(solution)/shard_map/ppermute | solution.py:12
  128.7 2.1 %collective-permute-done.15 = f32[4,16,8,1]{3,2,1,0:T(8,128)S(1)} collective-permute-done((f32[4,16,8,1]{3,2,1,0:T(8,128)S(1)}, f32[4,16,8,1]{3,2,1,0:T(8,128)S(1)}, u32[]{:S(2)}, u32[]{:S(2)}) %collective-permute-start.15) | collective-permute-done | bytes 2080 | tf_op jit(solution)/shard_map/ppermute | solution.py:12
  130.8 4.7 %collective-permute-done.20 = f32[4,16,8,1]{3,2,1,0:T(8,128)S(1)} collective-permute-done((f32[4,16,8,1]{3,2,1,0:T(8,128)S(1)}, f32[4,16,8,1]{3,2,1,0:T(8,128)S(1)}, u32[]{:S(2)}, u32[]{:S(2)}) %collective-permute-start.20) | collective-permute-done | bytes 2080 | tf_op jit(solution)/shard_map/ppermute | solution.py:12
  136.1 1.9 collective-permute-start.25
  138.2 1.9 collective-permute-start.26
  140.4 1.9 collective-permute-start.21
  142.3 2.1 %collective-permute-start.16 = (f32[4,16,8,1]{3,2,1,0:T(8,128)S(1)}, f32[4,16,8,1]{3,2,1,0:T(8,128)S(1)}, u32[]{:S(2)}, u32[]{:S(2)}) collective-permute-start(f32[4,16,8,1]{3,2,1,0:T(8,128)S(1)} %slice.589), channel_id=1, source_target_pairs={{0,1},{1,2},{2,3},{3,4},{4,5},{5,6},{6,7},{8,9},{9,10},{10,11},{11... | collective-permute-start | bytes 6152 | tf_op jit(solution)/shard_map/ppermute | solution.py:12
  144.4 7.3 %collective-permute-done.26 = f32[4,16,8,1]{3,2,1,0:T(8,128)S(1)} collective-permute-done((f32[4,16,8,1]{3,2,1,0:T(8,128)S(1)}, f32[4,16,8,1]{3,2,1,0:T(8,128)S(1)}, u32[]{:S(2)}, u32[]{:S(2)}) %collective-permute-start.26) | collective-permute-done | bytes 2080 | tf_op jit(solution)/shard_map/ppermute | solution.py:12
  151.7 0.8 multiply_add_fusion
  152.6 4.7 %collective-permute-start.27 = (f32[4,16,1,256]{3,2,1,0:T(1,128)S(1)}, f32[4,16,1,256]{3,2,1,0:T(1,128)S(1)}, u32[]{:S(2)}, u32[]{:S(2)}) collective-permute-start(f32[4,16,1,256]{3,2,1,0:T(1,128)S(1)} %slice.617), channel_id=1, source_target_pairs={{8,0},{16,8},{24,16},{32,24},{40,32},{48,40},{56,48},{64,56},{72,6... | collective-permute-start | bytes 196616 | tf_op jit(solution)/shard_map/ppermute | solution.py:12
  157.3 0.7 multiply_add_fusion.4
  158.1 1.9 collective-permute-start.22
  160.0 0.7 multiply_add_fusion.8
  160.8 3.3 %collective-permute-start.23 = (f32[4,16,8,1]{3,2,1,0:T(8,128)S(1)}, f32[4,16,8,1]{3,2,1,0:T(8,128)S(1)}, u32[]{:S(2)}, u32[]{:S(2)}) collective-permute-start(f32[4,16,8,1]{3,2,1,0:T(8,128)S(1)} %slice.608), channel_id=1, source_target_pairs={{1,0},{2,1},{3,2},{4,3},{5,4},{6,5},{7,6},{9,8},{10,9},{11,10},{12... | collective-permute-start | bytes 6152 | tf_op jit(solution)/shard_map/ppermute | solution.py:12
  164.1 2.9 %collective-permute-start.28 = (f32[4,16,8,1]{3,2,1,0:T(8,128)S(1)}, f32[4,16,8,1]{3,2,1,0:T(8,128)S(1)}, u32[]{:S(2)}, u32[]{:S(2)}) collective-permute-start(f32[4,16,8,1]{3,2,1,0:T(8,128)S(1)} %slice.620), channel_id=1, source_target_pairs={{1,0},{2,1},{3,2},{4,3},{5,4},{6,5},{7,6},{9,8},{10,9},{11,10},{12... | collective-permute-start | bytes 6152 | tf_op jit(solution)/shard_map/ppermute | solution.py:12
  167.6 4.2 %collective-permute-done.23 = f32[4,16,8,1]{3,2,1,0:T(8,128)S(1)} collective-permute-done((f32[4,16,8,1]{3,2,1,0:T(8,128)S(1)}, f32[4,16,8,1]{3,2,1,0:T(8,128)S(1)}, u32[]{:S(2)}, u32[]{:S(2)}) %collective-permute-start.23) | collective-permute-done | bytes 2080 | tf_op jit(solution)/shard_map/ppermute | solution.py:12
  171.8 5.2 %collective-permute-done.28 = f32[4,16,8,1]{3,2,1,0:T(8,128)S(1)} collective-permute-done((f32[4,16,8,1]{3,2,1,0:T(8,128)S(1)}, f32[4,16,8,1]{3,2,1,0:T(8,128)S(1)}, u32[]{:S(2)}, u32[]{:S(2)}) %collective-permute-start.28) | collective-permute-done | bytes 2080 | tf_op jit(solution)/shard_map/ppermute | solution.py:12
  178.0 1.9 collective-permute-start.29
  179.9 1.9 collective-permute-start.30
  182.0 1.9 collective-permute-start.24
  183.9 1.9 collective-permute-start.31
  185.8 1.2 pad_maximum_fusion.1
  187.1 8.0 %collective-permute-done.24 = f32[4,16,8,1]{3,2,1,0:T(8,128)S(1)} collective-permute-done((f32[4,16,8,1]{3,2,1,0:T(8,128)S(1)}, f32[4,16,8,1]{3,2,1,0:T(8,128)S(1)}, u32[]{:S(2)}, u32[]{:S(2)}) %collective-permute-start.24) | collective-permute-done | bytes 2080 | tf_op jit(solution)/shard_map/ppermute | solution.py:12
  195.2 1.0 subtract_bitcast_fusion.2
  196.2 1.0 subtract_bitcast_fusion.1
  197.2 2.4 %collective-permute-done.31 = f32[4,16,8,1]{3,2,1,0:T(8,128)S(1)} collective-permute-done((f32[4,16,8,1]{3,2,1,0:T(8,128)S(1)}, f32[4,16,8,1]{3,2,1,0:T(8,128)S(1)}, u32[]{:S(2)}, u32[]{:S(2)}) %collective-permute-start.31) | collective-permute-done | bytes 2080 | tf_op jit(solution)/shard_map/ppermute | solution.py:12
  199.5 1.1 subtract_bitcast_fusion
  200.7 1.3 copy.16
  (120 shorter events, 10.6 us)
Async XLA Ops:
  6.4 19.5 %copy-start.7 = (f32[8,2]{0,1:T(2,128)S(1)}, f32[8,2]{0,1:T(2,128)}, u32[]{:S(2)}) copy-start(f32[8,2]{0,1:T(2,128)} %param.13) | copy-start | bytes 196
  6.4 20.2 %copy-start.8 = (f32[8,2]{0,1:T(2,128)S(1)}, f32[8,2]{0,1:T(2,128)}, u32[]{:S(2)}) copy-start(f32[8,2]{0,1:T(2,128)} %param.14) | copy-start | bytes 196
  6.4 20.9 %copy-start.9 = (f32[8,2]{0,1:T(2,128)S(1)}, f32[8,2]{0,1:T(2,128)}, u32[]{:S(2)}) copy-start(f32[8,2]{0,1:T(2,128)} %param.15) | copy-start | bytes 196
  6.4 21.6 %copy-start.6 = (s32[16,8,256]{2,1,0:T(8,128)S(1)}, s32[16,8,256]{2,1,0:T(8,128)}, u32[]{:S(2)}) copy-start(s32[16,8,256]{2,1,0:T(8,128)} %param.11) | copy-start | bytes 393220
  8.1 30.2 %copy-start.1 = (f32[16,8,256]{2,1,0:T(8,128)S(1)}, f32[16,8,256]{2,1,0:T(8,128)}, u32[]{:S(2)}) copy-start(f32[16,8,256]{2,1,0:T(8,128)} %param.10) | copy-start | bytes 393220
  8.2 40.9 %collective-permute-start.3 = (f32[4,16,1,256]{3,2,1,0:T(1,128)S(1)}, f32[4,16,1,256]{3,2,1,0:T(1,128)S(1)}, u32[]{:S(2)}, u32[]{:S(2)}) collective-permute-start(f32[4,16,1,256]{3,2,1,0:T(1,128)S(1)} %slice.557), channel_id=1, source_target_pairs={{8,0},{16,8},{24,16},{32,24},{40,32},{48,40},{56,48},{64,56},{72,6... | collective-permute-start | bytes 196616 | tf_op jit(solution)/shard_map/ppermute | solution.py:12
  16.3 32.8 %collective-permute-start = (f32[4,16,1,256]{3,2,1,0:T(1,128)S(1)}, f32[4,16,1,256]{3,2,1,0:T(1,128)S(1)}, u32[]{:S(2)}, u32[]{:S(2)}) collective-permute-start(f32[4,16,1,256]{3,2,1,0:T(1,128)S(1)} %slice.550), channel_id=1, source_target_pairs={{8,0},{16,8},{24,16},{32,24},{40,32},{48,40},{56,48},{64,56},{72,6... | collective-permute-start | bytes 196616 | tf_op jit(solution)/shard_map/ppermute | solution.py:12
  18.9 30.2 %collective-permute-start.4 = (f32[4,16,8,1]{3,2,1,0:T(8,128)S(1)}, f32[4,16,8,1]{3,2,1,0:T(8,128)S(1)}, u32[]{:S(2)}, u32[]{:S(2)}) collective-permute-start(f32[4,16,8,1]{3,2,1,0:T(8,128)S(1)} %slice.560), channel_id=1, source_target_pairs={{1,0},{2,1},{3,2},{4,3},{5,4},{6,5},{7,6},{9,8},{10,9},{11,10},{12... | collective-permute-start | bytes 6152 | tf_op jit(solution)/shard_map/ppermute | solution.py:12
  23.2 25.9 %collective-permute-start.1 = (f32[4,16,8,1]{3,2,1,0:T(8,128)S(1)}, f32[4,16,8,1]{3,2,1,0:T(8,128)S(1)}, u32[]{:S(2)}, u32[]{:S(2)}) collective-permute-start(f32[4,16,8,1]{3,2,1,0:T(8,128)S(1)} %slice.552), channel_id=1, source_target_pairs={{1,0},{2,1},{3,2},{4,3},{5,4},{6,5},{7,6},{9,8},{10,9},{11,10},{12... | collective-permute-start | bytes 6152 | tf_op jit(solution)/shard_map/ppermute | solution.py:12
  49.7 14.6 %collective-permute-start.9 = (f32[4,16,1,256]{3,2,1,0:T(1,128)S(1)}, f32[4,16,1,256]{3,2,1,0:T(1,128)S(1)}, u32[]{:S(2)}, u32[]{:S(2)}) collective-permute-start(f32[4,16,1,256]{3,2,1,0:T(1,128)S(1)} %slice.572), channel_id=1, source_target_pairs={{0,8},{8,16},{16,24},{24,32},{32,40},{40,48},{48,56},{56,64},{64,7... | collective-permute-start | bytes 196616 | tf_op jit(solution)/shard_map/ppermute | solution.py:12
  51.8 12.6 %copy-start = (f32[4,3,16,8,256]{4,3,2,1,0:T(8,128)S(1)}, f32[4,3,16,8,256]{4,3,2,1,0:T(8,128)}, u32[]{:S(2)}) copy-start(f32[4,3,16,8,256]{4,3,2,1,0:T(8,128)} %param.9) | copy-start | bytes 4718596
  51.8 12.6 %collective-permute-start.10 = (f32[4,16,8,1]{3,2,1,0:T(8,128)S(1)}, f32[4,16,8,1]{3,2,1,0:T(8,128)S(1)}, u32[]{:S(2)}, u32[]{:S(2)}) collective-permute-start(f32[4,16,8,1]{3,2,1,0:T(8,128)S(1)} %slice.574), channel_id=1, source_target_pairs={{0,1},{1,2},{2,3},{3,4},{4,5},{5,6},{6,7},{8,9},{9,10},{10,11},{11... | collective-permute-start | bytes 6152 | tf_op jit(solution)/shard_map/ppermute | solution.py:12
  60.5 11.7 %collective-permute-start.5 = (f32[4,16,1,256]{3,2,1,0:T(1,128)S(1)}, f32[4,16,1,256]{3,2,1,0:T(1,128)S(1)}, u32[]{:S(2)}, u32[]{:S(2)}) collective-permute-start(f32[4,16,1,256]{3,2,1,0:T(1,128)S(1)} %slice.563), channel_id=1, source_target_pairs={{0,8},{8,16},{16,24},{24,32},{32,40},{40,48},{48,56},{56,64},{64,7... | collective-permute-start | bytes 196616 | tf_op jit(solution)/shard_map/ppermute | solution.py:12
  62.4 12.6 %collective-permute-start.2 = (f32[4,16,8,1]{3,2,1,0:T(8,128)S(1)}, f32[4,16,8,1]{3,2,1,0:T(8,128)S(1)}, u32[]{:S(2)}, u32[]{:S(2)}) collective-permute-start(f32[4,16,8,1]{3,2,1,0:T(8,128)S(1)} %slice.553), channel_id=1, source_target_pairs={{0,1},{1,2},{2,3},{3,4},{4,5},{5,6},{6,7},{8,9},{9,10},{10,11},{11... | collective-permute-start | bytes 6152 | tf_op jit(solution)/shard_map/ppermute | solution.py:12
  64.9 27.1 %collective-permute-start.11 = (f32[4,16,1,256]{3,2,1,0:T(1,128)S(1)}, f32[4,16,1,256]{3,2,1,0:T(1,128)S(1)}, u32[]{:S(2)}, u32[]{:S(2)}) collective-permute-start(f32[4,16,1,256]{3,2,1,0:T(1,128)S(1)} %slice.577), channel_id=1, source_target_pairs={{8,0},{16,8},{24,16},{32,24},{40,32},{48,40},{56,48},{64,56},{72,6... | collective-permute-start | bytes 196616 | tf_op jit(solution)/shard_map/ppermute | solution.py:12
  72.6 19.4 %collective-permute-start.6 = (f32[4,16,1,256]{3,2,1,0:T(1,128)S(1)}, f32[4,16,1,256]{3,2,1,0:T(1,128)S(1)}, u32[]{:S(2)}, u32[]{:S(2)}) collective-permute-start(f32[4,16,1,256]{3,2,1,0:T(1,128)S(1)} %slice.566), channel_id=1, source_target_pairs={{8,0},{16,8},{24,16},{32,24},{40,32},{48,40},{56,48},{64,56},{72,6... | collective-permute-start | bytes 196616 | tf_op jit(solution)/shard_map/ppermute | solution.py:12
  75.5 11.8 %collective-permute-start.7 = (f32[4,16,8,1]{3,2,1,0:T(8,128)S(1)}, f32[4,16,8,1]{3,2,1,0:T(8,128)S(1)}, u32[]{:S(2)}, u32[]{:S(2)}) collective-permute-start(f32[4,16,8,1]{3,2,1,0:T(8,128)S(1)} %slice.568), channel_id=1, source_target_pairs={{1,0},{2,1},{3,2},{4,3},{5,4},{6,5},{7,6},{9,8},{10,9},{11,10},{12... | collective-permute-start | bytes 6152 | tf_op jit(solution)/shard_map/ppermute | solution.py:12
  80.7 11.3 %collective-permute-start.12 = (f32[4,16,8,1]{3,2,1,0:T(8,128)S(1)}, f32[4,16,8,1]{3,2,1,0:T(8,128)S(1)}, u32[]{:S(2)}, u32[]{:S(2)}) collective-permute-start(f32[4,16,8,1]{3,2,1,0:T(8,128)S(1)} %slice.580), channel_id=1, source_target_pairs={{1,0},{2,1},{3,2},{4,3},{5,4},{6,5},{7,6},{9,8},{10,9},{11,10},{12... | collective-permute-start | bytes 6152 | tf_op jit(solution)/shard_map/ppermute | solution.py:12
  92.7 14.2 %collective-permute-start.17 = (f32[4,16,1,256]{3,2,1,0:T(1,128)S(1)}, f32[4,16,1,256]{3,2,1,0:T(1,128)S(1)}, u32[]{:S(2)}, u32[]{:S(2)}) collective-permute-start(f32[4,16,1,256]{3,2,1,0:T(1,128)S(1)} %slice.592), channel_id=1, source_target_pairs={{0,8},{8,16},{16,24},{24,32},{32,40},{40,48},{48,56},{56,64},{64,7... | collective-permute-start | bytes 196616 | tf_op jit(solution)/shard_map/ppermute | solution.py:12
  94.8 12.1 %collective-permute-start.18 = (f32[4,16,8,1]{3,2,1,0:T(8,128)S(1)}, f32[4,16,8,1]{3,2,1,0:T(8,128)S(1)}, u32[]{:S(2)}, u32[]{:S(2)}) collective-permute-start(f32[4,16,8,1]{3,2,1,0:T(8,128)S(1)} %slice.594), channel_id=1, source_target_pairs={{0,1},{1,2},{2,3},{3,4},{4,5},{5,6},{6,7},{8,9},{9,10},{10,11},{11... | collective-permute-start | bytes 6152 | tf_op jit(solution)/shard_map/ppermute | solution.py:12
  102.3 11.9 %collective-permute-start.13 = (f32[4,16,1,256]{3,2,1,0:T(1,128)S(1)}, f32[4,16,1,256]{3,2,1,0:T(1,128)S(1)}, u32[]{:S(2)}, u32[]{:S(2)}) collective-permute-start(f32[4,16,1,256]{3,2,1,0:T(1,128)S(1)} %slice.583), channel_id=1, source_target_pairs={{0,8},{8,16},{16,24},{24,32},{32,40},{40,48},{48,56},{56,64},{64,7... | collective-permute-start | bytes 196616 | tf_op jit(solution)/shard_map/ppermute | solution.py:12
  104.2 12.9 %collective-permute-start.8 = (f32[4,16,8,1]{3,2,1,0:T(8,128)S(1)}, f32[4,16,8,1]{3,2,1,0:T(8,128)S(1)}, u32[]{:S(2)}, u32[]{:S(2)}) collective-permute-start(f32[4,16,8,1]{3,2,1,0:T(8,128)S(1)} %slice.569), channel_id=1, source_target_pairs={{0,1},{1,2},{2,3},{3,4},{4,5},{5,6},{6,7},{8,9},{9,10},{10,11},{11... | collective-permute-start | bytes 6152 | tf_op jit(solution)/shard_map/ppermute | solution.py:12
  107.6 27.9 %collective-permute-start.19 = (f32[4,16,1,256]{3,2,1,0:T(1,128)S(1)}, f32[4,16,1,256]{3,2,1,0:T(1,128)S(1)}, u32[]{:S(2)}, u32[]{:S(2)}) collective-permute-start(f32[4,16,1,256]{3,2,1,0:T(1,128)S(1)} %slice.597), channel_id=1, source_target_pairs={{8,0},{16,8},{24,16},{32,24},{40,32},{48,40},{56,48},{64,56},{72,6... | collective-permute-start | bytes 196616 | tf_op jit(solution)/shard_map/ppermute | solution.py:12
  114.7 20.7 %collective-permute-start.14 = (f32[4,16,1,256]{3,2,1,0:T(1,128)S(1)}, f32[4,16,1,256]{3,2,1,0:T(1,128)S(1)}, u32[]{:S(2)}, u32[]{:S(2)}) collective-permute-start(f32[4,16,1,256]{3,2,1,0:T(1,128)S(1)} %slice.586), channel_id=1, source_target_pairs={{8,0},{16,8},{24,16},{32,24},{40,32},{48,40},{56,48},{64,56},{72,6... | collective-permute-start | bytes 196616 | tf_op jit(solution)/shard_map/ppermute | solution.py:12
  117.8 13.0 %collective-permute-start.15 = (f32[4,16,8,1]{3,2,1,0:T(8,128)S(1)}, f32[4,16,8,1]{3,2,1,0:T(8,128)S(1)}, u32[]{:S(2)}, u32[]{:S(2)}) collective-permute-start(f32[4,16,8,1]{3,2,1,0:T(8,128)S(1)} %slice.588), channel_id=1, source_target_pairs={{1,0},{2,1},{3,2},{4,3},{5,4},{6,5},{7,6},{9,8},{10,9},{11,10},{12... | collective-permute-start | bytes 6152 | tf_op jit(solution)/shard_map/ppermute | solution.py:12
  124.1 11.3 %collective-permute-start.20 = (f32[4,16,8,1]{3,2,1,0:T(8,128)S(1)}, f32[4,16,8,1]{3,2,1,0:T(8,128)S(1)}, u32[]{:S(2)}, u32[]{:S(2)}) collective-permute-start(f32[4,16,8,1]{3,2,1,0:T(8,128)S(1)} %slice.600), channel_id=1, source_target_pairs={{1,0},{2,1},{3,2},{4,3},{5,4},{6,5},{7,6},{9,8},{10,9},{11,10},{12... | collective-permute-start | bytes 6152 | tf_op jit(solution)/shard_map/ppermute | solution.py:12
  136.1 15.6 %collective-permute-start.25 = (f32[4,16,1,256]{3,2,1,0:T(1,128)S(1)}, f32[4,16,1,256]{3,2,1,0:T(1,128)S(1)}, u32[]{:S(2)}, u32[]{:S(2)}) collective-permute-start(f32[4,16,1,256]{3,2,1,0:T(1,128)S(1)} %slice.612), channel_id=1, source_target_pairs={{0,8},{8,16},{16,24},{24,32},{32,40},{40,48},{48,56},{56,64},{64,7... | collective-permute-start | bytes 196616 | tf_op jit(solution)/shard_map/ppermute | solution.py:12
  138.2 13.5 %collective-permute-start.26 = (f32[4,16,8,1]{3,2,1,0:T(8,128)S(1)}, f32[4,16,8,1]{3,2,1,0:T(8,128)S(1)}, u32[]{:S(2)}, u32[]{:S(2)}) collective-permute-start(f32[4,16,8,1]{3,2,1,0:T(8,128)S(1)} %slice.614), channel_id=1, source_target_pairs={{0,1},{1,2},{2,3},{3,4},{4,5},{5,6},{6,7},{8,9},{9,10},{10,11},{11... | collective-permute-start | bytes 6152 | tf_op jit(solution)/shard_map/ppermute | solution.py:12
  140.4 16.9 %collective-permute-start.21 = (f32[4,16,1,256]{3,2,1,0:T(1,128)S(1)}, f32[4,16,1,256]{3,2,1,0:T(1,128)S(1)}, u32[]{:S(2)}, u32[]{:S(2)}) collective-permute-start(f32[4,16,1,256]{3,2,1,0:T(1,128)S(1)} %slice.603), channel_id=1, source_target_pairs={{0,8},{8,16},{16,24},{24,32},{32,40},{40,48},{48,56},{56,64},{64,7... | collective-permute-start | bytes 196616 | tf_op jit(solution)/shard_map/ppermute | solution.py:12
  142.3 17.7 %collective-permute-start.16 = (f32[4,16,8,1]{3,2,1,0:T(8,128)S(1)}, f32[4,16,8,1]{3,2,1,0:T(8,128)S(1)}, u32[]{:S(2)}, u32[]{:S(2)}) collective-permute-start(f32[4,16,8,1]{3,2,1,0:T(8,128)S(1)} %slice.589), channel_id=1, source_target_pairs={{0,1},{1,2},{2,3},{3,4},{4,5},{5,6},{6,7},{8,9},{9,10},{10,11},{11... | collective-permute-start | bytes 6152 | tf_op jit(solution)/shard_map/ppermute | solution.py:12
  152.6 24.4 %collective-permute-start.27 = (f32[4,16,1,256]{3,2,1,0:T(1,128)S(1)}, f32[4,16,1,256]{3,2,1,0:T(1,128)S(1)}, u32[]{:S(2)}, u32[]{:S(2)}) collective-permute-start(f32[4,16,1,256]{3,2,1,0:T(1,128)S(1)} %slice.617), channel_id=1, source_target_pairs={{8,0},{16,8},{24,16},{32,24},{40,32},{48,40},{56,48},{64,56},{72,6... | collective-permute-start | bytes 196616 | tf_op jit(solution)/shard_map/ppermute | solution.py:12
  158.0 9.2 %copy-start.4 = (f32[4,16,8,256]{3,2,1,0:T(8,128)}, f32[4,16,8,256]{3,2,1,0:T(8,128)S(1)}, u32[]{:S(2)}) copy-start(f32[4,16,8,256]{3,2,1,0:T(8,128)S(1)} %multiply_add_fusion.4) | copy-start | bytes 1572868
  158.1 18.9 %collective-permute-start.22 = (f32[4,16,1,256]{3,2,1,0:T(1,128)S(1)}, f32[4,16,1,256]{3,2,1,0:T(1,128)S(1)}, u32[]{:S(2)}, u32[]{:S(2)}) collective-permute-start(f32[4,16,1,256]{3,2,1,0:T(1,128)S(1)} %slice.606), channel_id=1, source_target_pairs={{8,0},{16,8},{24,16},{32,24},{40,32},{48,40},{56,48},{64,56},{72,6... | collective-permute-start | bytes 196616 | tf_op jit(solution)/shard_map/ppermute | solution.py:12
  160.8 6.5 %copy-start.2 = (f32[4,16,8,256]{3,2,1,0:T(8,128)}, f32[4,16,8,256]{3,2,1,0:T(8,128)S(1)}, u32[]{:S(2)}) copy-start(f32[4,16,8,256]{3,2,1,0:T(8,128)S(1)} %multiply_add_fusion.8) | copy-start | bytes 1572868
  160.8 11.0 %collective-permute-start.23 = (f32[4,16,8,1]{3,2,1,0:T(8,128)S(1)}, f32[4,16,8,1]{3,2,1,0:T(8,128)S(1)}, u32[]{:S(2)}, u32[]{:S(2)}) collective-permute-start(f32[4,16,8,1]{3,2,1,0:T(8,128)S(1)} %slice.608), channel_id=1, source_target_pairs={{1,0},{2,1},{3,2},{4,3},{5,4},{6,5},{7,6},{9,8},{10,9},{11,10},{12... | collective-permute-start | bytes 6152 | tf_op jit(solution)/shard_map/ppermute | solution.py:12
  164.1 12.9 %collective-permute-start.28 = (f32[4,16,8,1]{3,2,1,0:T(8,128)S(1)}, f32[4,16,8,1]{3,2,1,0:T(8,128)S(1)}, u32[]{:S(2)}, u32[]{:S(2)}) collective-permute-start(f32[4,16,8,1]{3,2,1,0:T(8,128)S(1)} %slice.620), channel_id=1, source_target_pairs={{1,0},{2,1},{3,2},{4,3},{5,4},{6,5},{7,6},{9,8},{10,9},{11,10},{12... | collective-permute-start | bytes 6152 | tf_op jit(solution)/shard_map/ppermute | solution.py:12
  167.3 9.7 %copy-start.3 = (f32[4,16,8,256]{3,2,1,0:T(8,128)S(1)}, f32[4,16,8,256]{3,2,1,0:T(8,128)}, u32[]{:S(2)}) copy-start(f32[4,16,8,256]{3,2,1,0:T(8,128)} %copy-done.2) | copy-start | bytes 1572868
  167.3 9.7 %slice-start = ((f32[4,16,8,256]{3,2,1,0:T(8,128)}), f32[4,15,8,256]{3,2,1,0:T(8,128)S(1)}, s32[]{:S(2)}) async-start(f32[4,16,8,256]{3,2,1,0:T(8,128)} %copy-done.2), calls=%async_computation | async-start | bytes 983040 | tf_op jit(solution)/shard_map/slice | solution.py:17
  167.3 9.7 %copy-start.5 = (f32[4,16,8,256]{3,2,1,0:T(8,128)S(1)}, f32[4,16,8,256]{3,2,1,0:T(8,128)}, u32[]{:S(2)}) copy-start(f32[4,16,8,256]{3,2,1,0:T(8,128)} %copy-done.4) | copy-start | bytes 1572868
  167.4 9.7 %slice-start.1 = ((f32[4,16,8,256]{3,2,1,0:T(8,128)}), f32[4,15,8,256]{3,2,1,0:T(8,128)S(1)}, s32[]{:S(2)}) async-start(f32[4,16,8,256]{3,2,1,0:T(8,128)} %copy-done.4), calls=%async_computation.1 | async-start | bytes 983040 | tf_op jit(solution)/shard_map/slice | solution.py:17
  178.0 18.2 %collective-permute-start.29 = (f32[4,16,1,256]{3,2,1,0:T(1,128)S(1)}, f32[4,16,1,256]{3,2,1,0:T(1,128)S(1)}, u32[]{:S(2)}, u32[]{:S(2)}) collective-permute-start(f32[4,16,1,256]{3,2,1,0:T(1,128)S(1)} %slice.623), channel_id=1, source_target_pairs={{0,8},{8,16},{16,24},{24,32},{32,40},{40,48},{48,56},{56,64},{64,7... | collective-permute-start | bytes 196616 | tf_op jit(solution)/shard_map/ppermute | solution.py:12
  179.9 19.6 %collective-permute-start.30 = (f32[4,16,1,256]{3,2,1,0:T(1,128)S(1)}, f32[4,16,1,256]{3,2,1,0:T(1,128)S(1)}, u32[]{:S(2)}, u32[]{:S(2)}) collective-permute-start(f32[4,16,1,256]{3,2,1,0:T(1,128)S(1)} %slice.625), channel_id=1, source_target_pairs={{0,8},{8,16},{16,24},{24,32},{32,40},{40,48},{48,56},{56,64},{64,7... | collective-permute-start | bytes 196616 | tf_op jit(solution)/shard_map/ppermute | solution.py:12
  182.0 13.2 %collective-permute-start.24 = (f32[4,16,8,1]{3,2,1,0:T(8,128)S(1)}, f32[4,16,8,1]{3,2,1,0:T(8,128)S(1)}, u32[]{:S(2)}, u32[]{:S(2)}) collective-permute-start(f32[4,16,8,1]{3,2,1,0:T(8,128)S(1)} %slice.609), channel_id=1, source_target_pairs={{0,1},{1,2},{2,3},{3,4},{4,5},{5,6},{6,7},{8,9},{9,10},{10,11},{11... | collective-permute-start | bytes 6152 | tf_op jit(solution)/shard_map/ppermute | solution.py:12
  183.9 15.6 %collective-permute-start.31 = (f32[4,16,8,1]{3,2,1,0:T(8,128)S(1)}, f32[4,16,8,1]{3,2,1,0:T(8,128)S(1)}, u32[]{:S(2)}, u32[]{:S(2)}) collective-permute-start(f32[4,16,8,1]{3,2,1,0:T(8,128)S(1)} %slice.627), channel_id=1, source_target_pairs={{0,1},{1,2},{2,3},{3,4},{4,5},{5,6},{6,7},{8,9},{9,10},{10,11},{11... | collective-permute-start | bytes 6152 | tf_op jit(solution)/shard_map/ppermute | solution.py:12
where the time goes:
time: 204 us; the launch traced here: 202 us
  starting transfers between devices  99.9 us (49%)
  other arithmetic  48.7 us (24%)
  waiting for transfers between devices  42.3 us (21%)
  local copies, waits for them, and re-layouts  9.38 us (5%)
    ppermute x32, starting transfers between devices, from_behind(): lax.ppermute(value, axis, [(source, source + steps) for source in range(i...  99.9 us
    ppermute x32, waiting for transfers between devices, from_behind(): lax.ppermute(value, axis, [(source, source + steps) for source in range(i...  42.3 us
    mul x2, other arithmetic, run_steps(): state_v[pole] = [coef_b * state_u[pole][c] for c in range(3)]  10.3 us
    mul x2, other arithmetic, run_steps(): coef_a * state_u[pole][c] + state_v[pole][c] + coef_c * sectioned[c]  10.2 us
    select_n x2, other arithmetic, region_lookup(): value = jnp.where(region_ids == region, table[region, pole], value)  10.1 us
    add x9, other arithmetic, run_steps(): elec = [elec[c] + mask_float * residual[:, c] * scaled for c in range(3)]  5.32 us
    another operation x5, other arithmetic, run_steps(): return (jnp.stack(elec, 1), jnp.stack(magn, 1))  4.44 us
  transfers between devices with their start and end apart: 32, of which 10 were waited for; matrix products, arithmetic and copies ran while one was open for 22% of the time, Pallas kernels for 0%

commit v1 on v0

v1 whole, which is shorter than its diff:
```python
import functools

import jax
import jax.numpy as jnp
from jax import lax
from jax.experimental import pallas as pl
from jax.experimental.pallas import tpu as pltpu
from jax.sharding import PartitionSpec as P

MESH = pl.DeviceIdType.MESH
PORTS, NZ, ROWS, COLS = 4, 16, 8, 256
STEPS, REGIONS = 4, 8
LANES = 128
UNROLL = 4
OWN, HALO = 0, 1
FIELDS = 3 * PORTS + 2
NEIGHBOURS = [(1, 0), (-1, 0), (0, 1), (0, -1), (1, 1), (1, -1), (-1, 1), (-1, -1)]


def lane_tile(lt):
    return pl.ds(lt * LANES, LANES)


def kernel(
    residual, eps_inv, region_ids, source_mask, pole_a, pole_b, pole_c, waveform, plan,
    out_e, out_h,
    own_m, halo_m, ids, mask, consts, halo_consts, packed, recv_x, recv_y, recv_c,
    elec, magn, sect, coefs, strip_m, strip_e, strip_h, strip_s, strip_coefs,
    load_sem, send_sem, recv_sem,
):
    gx, gy = lax.axis_index("gx"), lax.axis_index("gy")
    size_x, size_y = lax.axis_size("gx"), lax.axis_size("gy")

    def there(dx, dy):
        x, y = gx + dx, gy + dy
        return (x >= 0) & (x < size_x) & (y >= 0) & (y < size_y)

    barrier = pltpu.get_barrier_semaphore()
    for dx, dy in NEIGHBOURS:
        @pl.when(there(dx, dy))
        def _(dx=dx, dy=dy):
            pl.semaphore_signal(
                barrier, inc=1, device_id=(gx + dx, gy + dy), device_id_type=MESH
            )

    loads = [
        pltpu.make_async_copy(source_mask, mask, load_sem.at[0]),
        pltpu.make_async_copy(residual, own_m, load_sem.at[1]),
        pltpu.make_async_copy(eps_inv, consts.at[0], load_sem.at[2]),
        pltpu.make_async_copy(region_ids, ids, load_sem.at[3]),
    ]
    for load in loads:
        load.start()

    lane = lax.broadcasted_iota(jnp.int32, (ROWS, LANES), 1)
    row = lax.broadcasted_iota(jnp.int32, (ROWS, LANES), 0)
    group = lax.rem(lane, 8)
    first_row, last_row = row == 0, row == ROWS - 1
    first_lane, last_lane = lane == 0, lane == LANES - 1
    first_z, last_z = lane < 8, lane >= LANES - 8
    left_cols = group < 4
    keep_low_x = (row < 4) | (gx > 0)
    keep_low_y = (group >= 4) | (gy > 0)
    zero = jnp.zeros((ROWS, LANES), jnp.float32)

    plane = jnp.zeros((4, COLS), jnp.float32)

    def clear_rows(lo):
        def body(z, carry):
            for p in range(PORTS):
                for c in range(3):
                    halo_m[p, c, z, lo:lo + 4, :] = plane
            for k in range(2):
                halo_consts[k, z, lo:lo + 4, :] = plane
            return carry

        lax.fori_loop(0, NZ, body, 0)
        recv_x[:, lo:lo + 4, :] = jnp.zeros((FIELDS, 4, LANES), jnp.float32)

    @pl.when(jnp.logical_not(there(1, 0)))
    def _():
        clear_rows(0)

    @pl.when(jnp.logical_not(there(-1, 0)))
    def _():
        clear_rows(4)

    for side, dy in ((0, -1), (1, 1)):
        @pl.when(jnp.logical_not(there(0, dy)))
        def _(side=side):
            recv_y[side] = jnp.zeros((FIELDS, ROWS, LANES), jnp.float32)

        for lo, dx in ((0, 1), (4, -1)):
            @pl.when(jnp.logical_not(there(dx, dy)))
            def _(side=side, lo=lo):
                recv_c[side, :, lo:lo + 4, :] = jnp.zeros((FIELDS, 4, LANES), jnp.float32)

    def clear_unsent(z, carry):
        for k in range(2):
            halo_consts[k, z, 3:5, :] = jnp.zeros((2, COLS), jnp.float32)
        return carry

    lax.fori_loop(0, NZ, clear_unsent, 0)
    for c in range(3):
        for rt in (OWN, HALO):
            elec[c, NZ, rt] = jnp.zeros((ROWS, COLS), jnp.float32)
            magn[c, 0, rt] = jnp.zeros((ROWS, COLS), jnp.float32)

    taps = [[], [], [], []]
    for region in range(REGIONS):
        total = [0.0, 0.0, 0.0, 0.0]
        for pole in range(2):
            a, b, c = pole_a[region, pole], pole_b[region, pole], pole_c[region, pole]
            u1 = c
            u2 = a * u1
            u3 = a * u2 + b * u1
            u4 = a * u3 + b * u2
            steps = (u1, u2 - u1, u3 - u2, u4 - u3)
            total = [total[j] + steps[j] for j in range(4)]
        for j in range(4):
            taps[j].append(total[j])

    def make_coefs(eps, region):
        hits = [region == jnp.float32(r) for r in range(REGIONS - 1)]
        result = [-0.25 * eps]
        for j in range(4):
            value = jnp.full((ROWS, LANES), taps[j][REGIONS - 1], jnp.float32)
            for r in range(REGIONS - 1):
                value = jnp.where(hits[r], taps[j][r], value)
            result.append(1.0 - eps * value if j == 0 else eps * value)
        return result

    for load in loads:
        load.wait()

    for f in range(FIELDS):
        packed[f] = zero

    def prepare(z, carry):
        at_z = (lane >= 8 * z) & (lane < 8 * z + 8)
        for lt in range(2):
            consts[1, z, :, lane_tile(lt)] = ids[z, :, lane_tile(lt)].astype(jnp.float32)
        weight = [mask[z, :, lane_tile(lt)].astype(jnp.float32) for lt in range(2)]
        for f in range(FIELDS):
            if f < 3 * PORTS:
                p, c = f // 3, f % 3
                tiles = []
                for lt in range(2):
                    value = own_m[p, c, z, :, lane_tile(lt)] * weight[lt]
                    own_m[p, c, z, :, lane_tile(lt)] = value
                    tiles.append(value)
            else:
                tiles = [consts[f - 3 * PORTS, z, :, lane_tile(lt)] for lt in range(2)]
            edge = jnp.where(lane < 4, tiles[0], tiles[1])
            packed[f] = jnp.where(at_z, pltpu.roll(edge, lax.rem(8 * z + 4, LANES), 1), packed[f])
        return carry

    lax.fori_loop(0, NZ, prepare, 0)

    peers = 0
    for dx, dy in NEIGHBOURS:
        peers = peers + jnp.where(there(dx, dy), 1, 0)
    pl.semaphore_wait(barrier, peers)

    def remote(index, src, dst, dx, dy):
        return pltpu.make_async_remote_copy(
            src_ref=src, dst_ref=dst, send_sem=send_sem.at[index], recv_sem=recv_sem.at[index],
            device_id=(gx + dx, gy + dy), device_id_type=MESH,
        )

    def rows_of(dx):
        return pl.ds(4, 4) if dx > 0 else pl.ds(0, 4)

    def port_copy(p, dx):
        side = 0 if dx > 0 else 1
        return remote(
            16 + 2 * p + side, own_m.at[p, :, :, rows_of(dx), :],
            halo_m.at[p, :, :, rows_of(dx), :], dx, 0,
        )

    edge_copies = []
    for dx in (1, -1):
        rows = pl.ds(5, 3) if dx > 0 else pl.ds(0, 3)
        edge_copies.append((dx, 0, remote(
            len(edge_copies), consts.at[:, :, rows, :], halo_consts.at[:, :, rows, :], dx, 0)))
    for dx, dy in NEIGHBOURS:
        if dy == 0:
            src, dst = packed.at[:, rows_of(dx), :], recv_x.at[:, rows_of(dx), :]
        elif dx == 0:
            src, dst = packed, recv_y.at[0 if dy > 0 else 1]
        else:
            src = packed.at[:, rows_of(dx), :]
            dst = recv_c.at[0 if dy > 0 else 1, :, rows_of(dx), :]
        edge_copies.append((dx, dy, remote(len(edge_copies), src, dst, dx, dy)))

    for dx, dy, copy in edge_copies:
        @pl.when(there(dx, dy))
        def _(copy=copy):
            copy.start()
    for p in range(PORTS):
        for dx in (1, -1):
            @pl.when(there(dx, 0))
            def _(p=p, dx=dx):
                port_copy(p, dx).start()

    def coef_rows(source, rt):
        def body(z, carry):
            for lt in range(2):
                values = make_coefs(source[0, z, :, lane_tile(lt)], source[1, z, :, lane_tile(lt)])
                for k in range(5):
                    coefs[k, z, rt, :, lane_tile(lt)] = values[k]
            return carry

        lax.fori_loop(0, NZ, body, 0)

    coef_rows(consts, OWN)
    for dx, dy, copy in edge_copies:
        @pl.when(there(-dx, -dy))
        def _(copy=copy):
            copy.wait_recv()
    coef_rows(halo_consts, HALO)
    for rt, source in ((OWN, recv_y), (HALO, recv_c)):
        for f in range(FIELDS - 2):
            strip_m[rt, f] = jnp.where(left_cols, source[0, f], source[1, f])
        eps, region = [
            jnp.where(left_cols, source[0, f], source[1, f]) for f in (FIELDS - 2, FIELDS - 1)
        ]
        values = make_coefs(eps, region)
        for k in range(5):
            strip_coefs[rt, k] = values[k]

    def up_row(values):
        rolled = [pltpu.roll(value, ROWS - 1, 0) for value in values]
        return [
            jnp.where(last_row, rolled[1 - rt], rolled[rt]) for rt in (OWN, HALO)
        ]

    def down_row(values):
        rolled = [pltpu.roll(value, 1, 0) for value in values]
        return [
            jnp.where(first_row, rolled[1 - rt], rolled[rt]) for rt in (OWN, HALO)
        ]

    def up_col(tiles, inserted):
        rolled = [pltpu.roll(tile, LANES - 1, 1) for tile in tiles]
        return [
            jnp.where(last_lane, rolled[1], rolled[0]),
            jnp.where(last_lane, inserted, rolled[1]),
        ]

    def down_col(tiles, inserted):
        rolled = [pltpu.roll(tile, 1, 1) for tile in tiles]
        return [
            jnp.where(first_lane, inserted, rolled[0]),
            jnp.where(first_lane, rolled[0], rolled[1]),
        ]

    both = (OWN, HALO)

    def strip_up_z(value):
        return jnp.where(last_z, 0.0, pltpu.roll(value, LANES - 8, 1))

    def strip_down_z(value):
        return jnp.where(first_z, 0.0, pltpu.roll(value, 8, 1))

    def strip_magnetic(s, gathered):
        ex, ey, ez = [[strip_e[rt, c] for rt in both] for c in range(3)]
        ey_up, ez_up = up_row(ey), up_row(ez)
        for rt in both:
            ex_next = jnp.where(group == 3, gathered[rt][0], pltpu.roll(ex[rt], LANES - 1, 1))
            ez_next = jnp.where(group == 3, gathered[rt][1], pltpu.roll(ez[rt], LANES - 1, 1))
            curls = (
                (ez_next - ez[rt]) - (strip_up_z(ey[rt]) - ey[rt]),
                (strip_up_z(ex[rt]) - ex[rt]) - (ez_up[rt] - ez[rt]),
                (ey_up[rt] - ey[rt]) - (ex_next - ex[rt]),
            )
            for c in range(3):
                value = curls[c] if s == 0 else strip_h[rt, c] + curls[c]
                if c != 1:
                    value = jnp.where(keep_low_y, value, 0.0)
                if c != 0 and rt == HALO:
                    value = jnp.where(keep_low_x, value, 0.0)
                strip_h[rt, c] = value

    def strip_electric(p, s, gathered, amplitude):
        hx, hy, hz = [[strip_h[rt, c] for rt in both] for c in range(3)]
        hy_down, hz_down = down_row(hy), down_row(hz)
        for rt in both:
            hx_prev = jnp.where(group == 4, gathered[rt][0], pltpu.roll(hx[rt], 1, 1))
            hz_prev = jnp.where(group == 4, gathered[rt][1], pltpu.roll(hz[rt], 1, 1))
            backs = (
                (hz[rt] - hz_prev) - (hy[rt] - strip_down_z(hy[rt])),
                (hx[rt] - strip_down_z(hx[rt])) - (hz[rt] - hz_down[rt]),
                (hy[rt] - hy_down[rt]) - (hx[rt] - hx_prev),
            )
            for c in range(3):
                value = strip_e[rt, c] + strip_coefs[rt, 0] * backs[c]
                strip_s[s, rt, c] = value
                new = strip_coefs[rt, 1] * value
                for j in range(1, s + 1):
                    new = new - strip_coefs[rt, 1 + j] * strip_s[s - j, rt, c]
                strip_e[rt, c] = new + strip_m[rt, 3 * p + c] * amplitude

    def cell_pass(p, s, amplitude):
        last = s == STEPS - 1

        def one_plane(z, gathered):
            (col_hx, col_hz), (col_ex, col_ez) = gathered
            el = [[[elec[c, z, rt, :, lane_tile(lt)] for lt in range(2)] for rt in both] for c in range(3)]
            up_z = [[[elec[c, z + 1, rt, :, lane_tile(lt)] for lt in range(2)] for rt in both] for c in range(2)]
            ex, ey, ez = el
            turn = lax.rem(251 - 8 * z, LANES)
            ey_xn = [up_row([ey[rt][lt] for rt in both]) for lt in range(2)]
            ez_xn = [up_row([ez[rt][lt] for rt in both]) for lt in range(2)]
            mags = [[[None] * 2 for _ in both] for _ in range(3)]
            for rt in both:
                ex_yn = up_col(ex[rt], pltpu.roll(strip_e[rt, 0], turn, 1))
                ez_yn = up_col(ez[rt], pltpu.roll(strip_e[rt, 2], turn, 1))
                for lt in range(2):
                    curls = (
                        (ez_yn[lt] - ez[rt][lt]) - (up_z[1][rt][lt] - ey[rt][lt]),
                        (up_z[0][rt][lt] - ex[rt][lt]) - (ez_xn[lt][rt] - ez[rt][lt]),
                        (ey_xn[lt][rt] - ey[rt][lt]) - (ex_yn[lt] - ex[rt][lt]),
                    )
                    for c in range(3):
                        if last and rt == HALO and c == 0:
                            continue
                        value = curls[c]
                        if s > 0:
                            value = magn[c, z + 1, rt, :, lane_tile(lt)] + value
                        if rt == HALO and c != 0:
                            value = jnp.where(keep_low_x, value, 0.0)
                        magn[c, z + 1, rt, :, lane_tile(lt)] = value
                        mags[c][rt][lt] = value
                        if last and rt == OWN:
                            out_h[p, c, z, :, lane_tile(lt)] = -0.5 * value
            hx, hy, hz = mags
            hy_xp = [down_row([hy[rt][lt] for rt in both]) for lt in range(2)]
            hz_xp = [down_row([hz[rt][lt] for rt in both]) for lt in range(2)]
            turn = lax.rem(253 - 8 * z, LANES)
            col_hx, col_hz, col_ex, col_ez = list(col_hx), list(col_hz), list(col_ex), list(col_ez)
            for rt in both:
                if last and rt == HALO:
                    continue
                hx_yp = down_col(hx[rt], pltpu.roll(strip_h[rt, 0], turn, 1))
                hz_yp = down_col(hz[rt], pltpu.roll(strip_h[rt, 2], turn, 1))
                if not last:
                    at = lane == 8 * z + 4
                    by = lax.rem(8 * z + 5, LANES)
                    col_hx[rt] = jnp.where(at, pltpu.roll(hx[rt][1], by, 1), col_hx[rt])
                    col_hz[rt] = jnp.where(at, pltpu.roll(hz[rt][1], by, 1), col_hz[rt])
                for lt in range(2):
                    hx_zp = magn[0, z, rt, :, lane_tile(lt)]
                    hy_zp = magn[1, z, rt, :, lane_tile(lt)]
                    backs = (
                        (hz[rt][lt] - hz_yp[lt]) - (hy[rt][lt] - hy_zp),
                        (hx[rt][lt] - hx_zp) - (hz[rt][lt] - hz_xp[lt][rt]),
                        (hy[rt][lt] - hy_xp[lt][rt]) - (hx[rt][lt] - hx_yp[lt]),
                    )
                    factors = [coefs[k, z, rt, :, lane_tile(lt)] for k in range(2 + s)]
                    source = own_m if rt == OWN else halo_m
                    for c in range(3):
                        value = el[c][rt][lt] + factors[0] * backs[c]
                        new = factors[1] * value
                        for j in range(1, s + 1):
                            new = new - factors[1 + j] * sect[s - j, c, z, rt, :, lane_tile(lt)]
                        if last:
                            out_e[p, c, z, :, lane_tile(lt)] = new
                            continue
                        new = new + source[p, c, z, :, lane_tile(lt)] * amplitude
                        sect[s, c, z, rt, :, lane_tile(lt)] = value
                        elec[c, z, rt, :, lane_tile(lt)] = new
                        if lt == 0 and c != 1:
                            at = lane == 8 * z + 3
                            rolled = pltpu.roll(new, lax.rem(8 * z + 3, LANES), 1)
                            if c == 0:
                                col_ex[rt] = jnp.where(at, rolled, col_ex[rt])
                            else:
                                col_ez[rt] = jnp.where(at, rolled, col_ez[rt])
            return ((tuple(col_hx), tuple(col_hz)), (tuple(col_ex), tuple(col_ez)))

        def body(block, gathered):
            for offset in range(UNROLL):
                gathered = one_plane(block * UNROLL + offset, gathered)
            return gathered

        start = (((zero, zero), (zero, zero)), ((zero, zero), (zero, zero)))
        if last:
            start = (((0, 0), (0, 0)), ((0, 0), (0, 0)))
        return lax.fori_loop(0, NZ // UNROLL, body, start)

    def port_body(p, carry):
        amplitude = [waveform[plan[s], p] for s in range(STEPS)]
        gathered = [
            [
                pltpu.roll(source[3 * p + c], LANES - 1, 1) * amplitude[0]
                for c in (0, 2)
            ]
            for source in (packed, recv_x)
        ]
        for rt in both:
            for c in range(3):
                strip_e[rt, c] = strip_m[rt, 3 * p + c] * amplitude[0]
        for dx in (1, -1):
            @pl.when(there(-dx, 0))
            def _(dx=dx):
                port_copy(p, dx).wait_recv()

        def first_source(z, inner):
            for rt, source in ((OWN, own_m), (HALO, halo_m)):
                for c in range(3):
                    for lt in range(2):
                        elec[c, z, rt, :, lane_tile(lt)] = source[p, c, z, :, lane_tile(lt)] * amplitude[0]
            return inner

        lax.fori_loop(0, NZ, first_source, 0)
        for s in range(STEPS):
            strip_magnetic(s, gathered)
            after = amplitude[min(s + 1, STEPS - 1)]
            (col_hx, col_hz), (col_ex, col_ez) = cell_pass(p, s, after)
            if s < STEPS - 1:
                strip_electric(p, s, [[col_hx[rt], col_hz[rt]] for rt in both], after)
                gathered = [[col_ex[rt], col_ez[rt]] for rt in both]
        return carry

    lax.fori_loop(0, PORTS, port_body, 0)

    for dx, dy, copy in edge_copies:
        @pl.when(there(dx, dy))
        def _(copy=copy):
            copy.wait_send()
    for p in range(PORTS):
        for dx in (1, -1):
            @pl.when(there(dx, 0))
            def _(p=p, dx=dx):
                port_copy(p, dx).wait_send()


def local(residual, eps_inv, region_ids, source_mask, pole_a, pole_b, pole_c, waveform, plan):
    hbm = pl.BlockSpec(memory_space=pl.ANY)
    smem = pl.BlockSpec(memory_space=pltpu.SMEM)
    vmem = pl.BlockSpec(memory_space=pltpu.VMEM)
    shape = (PORTS, 3, NZ, ROWS, COLS)
    f32 = jnp.float32
    return pl.pallas_call(
        kernel,
        out_shape=[jax.ShapeDtypeStruct(shape, f32)] * 2,
        in_specs=[hbm] * 4 + [smem] * 5,
        out_specs=[vmem] * 2,
        scratch_shapes=[
            pltpu.VMEM(shape, f32),
            pltpu.VMEM(shape, f32),
            pltpu.VMEM((NZ, ROWS, COLS), jnp.int32),
            pltpu.VMEM((NZ, ROWS, COLS), jnp.int32),
            pltpu.VMEM((2, NZ, ROWS, COLS), f32),
            pltpu.VMEM((2, NZ, ROWS, COLS), f32),
            pltpu.VMEM((FIELDS, ROWS, LANES), f32),
            pltpu.VMEM((FIELDS, ROWS, LANES), f32),
            pltpu.VMEM((2, FIELDS, ROWS, LANES), f32),
            pltpu.VMEM((2, FIELDS, ROWS, LANES), f32),
            pltpu.VMEM((3, NZ + 1, 2, ROWS, COLS), f32),
            pltpu.VMEM((3, NZ + 1, 2, ROWS, COLS), f32),
            pltpu.VMEM((STEPS - 1, 3, NZ, 2, ROWS, COLS), f32),
            pltpu.VMEM((5, NZ, 2, ROWS, COLS), f32),
            pltpu.VMEM((2, 3 * PORTS, ROWS, LANES), f32),
            pltpu.VMEM((2, 3, ROWS, LANES), f32),
            pltpu.VMEM((2, 3, ROWS, LANES), f32),
            pltpu.VMEM((STEPS - 1, 2, 3, ROWS, LANES), f32),
            pltpu.VMEM((2, 5, ROWS, LANES), f32),
            pltpu.SemaphoreType.DMA((4,)),
            pltpu.SemaphoreType.DMA((16 + 2 * PORTS,)),
            pltpu.SemaphoreType.DMA((16 + 2 * PORTS,)),
        ],
        compiler_params=pltpu.CompilerParams(
            collective_id=0, has_side_effects=True, vmem_limit_bytes=40 << 20
        ),
        cost_estimate=pl.CostEstimate(flops=60000000, bytes_accessed=5242880, transcendentals=0),
    )(residual, eps_inv, region_ids, source_mask, pole_a, pole_b, pole_c, waveform, plan)


def solution(mesh):
    cells = P(None, "gx", "gy")
    fields = P(None, None, None, "gx", "gy")
    return jax.shard_map(
        local,
        mesh=mesh,
        in_specs=(fields, cells, cells, cells, P(), P(), P(), P(), P()),
        out_specs=(fields, fields),
        check_vma=False,
    )
```

time: 204 us -> 51 us (0.25)
  the two profiles are of different devices: /device:TPU:6 before, /device:TPU:231 now
where the time goes in v1:
time: 51 us; the launch traced here: 50.8 us
  Pallas kernels  40 us (78%)
  local copies, waits for them, and re-layouts  10.1 us (20%)
  between operations  0.65 us (1%)
    pallas_call x1, Pallas kernels, local(): pl.pallas_call(kernel, out_shape=[jax.ShapeDtypeStruct(shape, f32)] * 2,...  40 us
    unnamed x16, local copies, waits for them, and re-layouts  10.1 us

profile of v1, /device:TPU:231, one launch (start us, length us, event | category | flops | bytes accessed | tf_op | source)
XLA Modules:
  0.0 50.8 jit_solution(10363703781440608667)
XLA Ops:
  0.6 0.8 %copy.11.pole_a = f32[8,2]{1,0:T(8,128)S(1)} copy(f32[8,2]{0,1:T(2,128)} %param.13) | data formatting | bytes 128 | tf_op args[4]
  1.4 0.8 %copy.12.pole_b = f32[8,2]{1,0:T(8,128)S(1)} copy(f32[8,2]{0,1:T(2,128)} %param.14) | data formatting | bytes 128 | tf_op args[5]
  2.1 0.8 %copy.13.pole_c = f32[8,2]{1,0:T(8,128)S(1)} copy(f32[8,2]{0,1:T(2,128)} %param.15) | data formatting | bytes 128 | tf_op args[6]
  2.9 0.8 %copy.14.waveform = f32[64,4]{1,0:T(8,128)S(1)} copy(f32[64,4]{0,1:T(4,128)} %param.16) | data formatting | bytes 2048 | tf_op args[7]
  3.7 0.0 copy-start
  3.7 1.4 %copy-done = f32[4,3,16,8,256]{4,3,2,1,0:T(8,128)S(1)} copy-done((f32[4,3,16,8,256]{4,3,2,1,0:T(8,128)S(1)}, f32[4,3,16,8,256]{4,3,2,1,0:T(8,128)}, u32[]{:S(2)}) %copy-start) | copy-done | bytes 1572888
  5.1 0.0 copy-start.1
  5.1 0.9 %copy-done.1 = f32[16,8,256]{2,1,0:T(8,128)S(1)} copy-done((f32[16,8,256]{2,1,0:T(8,128)S(1)}, f32[16,8,256]{2,1,0:T(8,128)}, u32[]{:S(2)}) %copy-start.1) | copy-done | bytes 131096
  6.0 0.0 copy-start.2
  6.0 0.9 %copy-done.2 = s32[16,8,256]{2,1,0:T(8,128)S(1)} copy-done((s32[16,8,256]{2,1,0:T(8,128)S(1)}, s32[16,8,256]{2,1,0:T(8,128)}, u32[]{:S(2)}) %copy-start.2) | copy-done | bytes 131096
  6.9 0.0 copy-start.3
  6.9 0.9 %copy-done.3 = s32[16,8,256]{2,1,0:T(8,128)S(1)} copy-done((s32[16,8,256]{2,1,0:T(8,128)S(1)}, s32[16,8,256]{2,1,0:T(8,128)}, u32[]{:S(2)}) %copy-start.3) | copy-done | bytes 131096
  7.8 0.0 copy-start.4
  7.8 0.7 %copy-done.4 = s32[4]{0:T(128)S(1)} copy-done((s32[4]{0:T(128)S(1)}, s32[4]{0:T(128)}, u32[]{:S(2)}) %copy-start.4) | copy-done | bytes 40
  8.4 40.0 %shard_map.104 = (f32[4,3,16,8,256]{4,3,2,1,0:T(8,128)S(1)}, f32[4,3,16,8,256]{4,3,2,1,0:T(8,128)S(1)}) custom-call(f32[4,3,16,8,256]{4,3,2,1,0:T(8,128)S(1)} %copy-done, f32[16,8,256]{2,1,0:T(8,128)S(1)} %copy-done.1, s32[16,8,256]{2,1,0:T(8,128)S(1)} %copy-done.2, s32[16,8,256]{2,1,0:T(8,128)S(1)} %copy-done.3, f32[8,2]{1,0:T(8,128)S(1)} %copy.11.pole_a, ...), custom_call_target="tpu_custom_call" | custom-call | flops 60000000 | bytes 5242880 | tf_op jit(solution)/shard_map/pallas_call | solution.py:445
  48.5 1.1 %copy.17 = f32[4,3,16,8,256]{4,3,2,1,0:T(8,128)} copy(f32[4,3,16,8,256]{4,3,2,1,0:T(8,128)S(1)} %get-tuple-element.4) | data formatting | bytes 3145728
  49.6 1.1 %copy.18 = f32[4,3,16,8,256]{4,3,2,1,0:T(8,128)} copy(f32[4,3,16,8,256]{4,3,2,1,0:T(8,128)S(1)} %get-tuple-element.5) | data formatting | bytes 3145728
Async XLA Ops:
  3.7 1.4 %copy-start = (f32[4,3,16,8,256]{4,3,2,1,0:T(8,128)S(1)}, f32[4,3,16,8,256]{4,3,2,1,0:T(8,128)}, u32[]{:S(2)}) copy-start(f32[4,3,16,8,256]{4,3,2,1,0:T(8,128)} %residual.1) | copy-start | bytes 4718596
  5.1 0.9 %copy-start.1 = (f32[16,8,256]{2,1,0:T(8,128)S(1)}, f32[16,8,256]{2,1,0:T(8,128)}, u32[]{:S(2)}) copy-start(f32[16,8,256]{2,1,0:T(8,128)} %eps_inv.1) | copy-start | bytes 393220
  6.0 0.9 %copy-start.2 = (s32[16,8,256]{2,1,0:T(8,128)S(1)}, s32[16,8,256]{2,1,0:T(8,128)}, u32[]{:S(2)}) copy-start(s32[16,8,256]{2,1,0:T(8,128)} %region_ids.1) | copy-start | bytes 393220
  6.9 0.9 %copy-start.3 = (s32[16,8,256]{2,1,0:T(8,128)S(1)}, s32[16,8,256]{2,1,0:T(8,128)}, u32[]{:S(2)}) copy-start(s32[16,8,256]{2,1,0:T(8,128)} %source_mask.1) | copy-start | bytes 393220
  7.8 0.7 %copy-start.4 = (s32[4]{0:T(128)S(1)}, s32[4]{0:T(128)}, u32[]{:S(2)}) copy-start(s32[4]{0:T(128)} %plan.1) | copy-start | bytes 52

commit v2 on v1

v2 whole, which is shorter than its diff:
```python
import functools

import jax
import jax.numpy as jnp
from jax import lax
from jax.experimental import pallas as pl
from jax.experimental.pallas import tpu as pltpu
from jax.sharding import PartitionSpec as P

MESH = pl.DeviceIdType.MESH
PORTS, NZ, ROWS, COLS = 4, 16, 8, 256
STEPS, REGIONS = 4, 8
UNROLL = 8
LANES = 128
OWN, HALO = 0, 1
LEFT, RIGHT = 0, 1
FIELDS = 3 * PORTS + 2
NEIGHBOURS = [(1, 0), (-1, 0), (0, 1), (0, -1), (1, 1), (1, -1), (-1, 1), (-1, -1)]
EDGE_ORDER = NEIGHBOURS[4:] + NEIGHBOURS[2:4] + NEIGHBOURS[:2]


def lane_tile(lt):
    return pl.ds(lt * LANES, LANES)


def kernel(
    residual, eps_inv, region_ids, source_mask, pole_a_in, pole_b_in, pole_c_in, waveform_in, plan_in,
    out_e, out_h,
    pole_a, pole_b, pole_c, waveform, plan, own_m, halo_m, ids, mask, consts, halo_consts, packed, recv_x, recv_y, recv_c,
    elec_0, elec_1, magn_0, magn_1, sect_0, sect_1, sect_2, coefs, strip_m, strip_coefs, edge_e, edge_h, insert_e, insert_h,
    load_sem, send_sem, recv_sem,
):
    gx, gy = lax.axis_index("gx"), lax.axis_index("gy")
    elecs, magns, sects = (elec_0, elec_1), (magn_0, magn_1), (sect_0, sect_1, sect_2)
    size_x, size_y = lax.axis_size("gx"), lax.axis_size("gy")

    def there(dx, dy):
        x, y = gx + dx, gy + dy
        return (x >= 0) & (x < size_x) & (y >= 0) & (y < size_y)

    barrier = pltpu.get_barrier_semaphore()
    for dx, dy in NEIGHBOURS:
        @pl.when(there(dx, dy))
        def _(dx=dx, dy=dy):
            pl.semaphore_signal(
                barrier, inc=1, device_id=(gx + dx, gy + dy), device_id_type=MESH
            )

    loads = [
        pltpu.make_async_copy(source_mask, mask, load_sem.at[0]),
        pltpu.make_async_copy(residual, own_m.at[:, :, pl.ds(0, NZ)], load_sem.at[1]),
        pltpu.make_async_copy(eps_inv, consts.at[0], load_sem.at[2]),
        pltpu.make_async_copy(region_ids, ids, load_sem.at[3]),
    ]
    small = (
        (pole_a_in, pole_a), (pole_b_in, pole_b), (pole_c_in, pole_c),
        (waveform_in, waveform), (plan_in, plan),
    )
    small_loads = [
        pltpu.make_async_copy(source, target, load_sem.at[4 + index])
        for index, (source, target) in enumerate(small)
    ]
    loads = loads + small_loads
    for load in loads:
        load.start()

    lane = lax.broadcasted_iota(jnp.int32, (ROWS, LANES), 1)
    row = lax.broadcasted_iota(jnp.int32, (ROWS, LANES), 0)
    group = lax.rem(lane, 8)
    first_row, last_row = row == 0, row == ROWS - 1
    first_lane, last_lane = lane == 0, lane == LANES - 1
    first_z, last_z = lane < 8, lane >= LANES - 8
    left_cols = group < 4
    keep_low_x = (row < 4) | (gx > 0)
    keep_low_y = (group >= 4) | (gy > 0)
    zero = jnp.zeros((ROWS, LANES), jnp.float32)

    plane = jnp.zeros((4, COLS), jnp.float32)

    def clear_rows(lo):
        def body(z, carry):
            for p in range(PORTS):
                for c in range(3):
                    halo_m[p, c, z, lo:lo + 4, :] = plane
            for k in range(2):
                halo_consts[k, z, lo:lo + 4, :] = plane
            return carry

        lax.fori_loop(0, NZ, body, 0)
        recv_x[:, lo:lo + 4, :] = jnp.zeros((FIELDS, 4, LANES), jnp.float32)

    @pl.when(jnp.logical_not(there(1, 0)))
    def _():
        clear_rows(0)

    @pl.when(jnp.logical_not(there(-1, 0)))
    def _():
        clear_rows(4)

    for side, dy in ((0, -1), (1, 1)):
        @pl.when(jnp.logical_not(there(0, dy)))
        def _(side=side):
            recv_y[side] = jnp.zeros((FIELDS, ROWS, LANES), jnp.float32)

        for lo, dx in ((0, 1), (4, -1)):
            @pl.when(jnp.logical_not(there(dx, dy)))
            def _(side=side, lo=lo):
                recv_c[side, :, lo:lo + 4, :] = jnp.zeros((FIELDS, 4, LANES), jnp.float32)

    def clear_unsent(z, carry):
        for k in range(2):
            halo_consts[k, z, 3:5, :] = jnp.zeros((2, COLS), jnp.float32)
        return carry

    lax.fori_loop(0, NZ, clear_unsent, 0)
    for p in range(PORTS):
        for c in range(2):
            own_m[p, c, NZ] = jnp.zeros((ROWS, COLS), jnp.float32)
            halo_m[p, c, NZ] = jnp.zeros((ROWS, COLS), jnp.float32)
    for ref in elecs:
        for c in range(2):
            for rt in (OWN, HALO):
                ref[c, NZ, rt] = jnp.zeros((ROWS, COLS), jnp.float32)

    for load in small_loads:
        load.wait()

    taps = [[], [], [], []]
    for region in range(REGIONS):
        total = [0.0, 0.0, 0.0, 0.0]
        for pole in range(2):
            a, b, c = pole_a[pole, region], pole_b[pole, region], pole_c[pole, region]
            u1 = c
            u2 = a * u1
            u3 = a * u2 + b * u1
            u4 = a * u3 + b * u2
            steps = (u1, u2 - u1, u3 - u2, u4 - u3)
            total = [total[j] + steps[j] for j in range(4)]
        for j in range(4):
            taps[j].append(total[j])

    def make_coefs(eps, region):
        hits = [region == jnp.float32(r) for r in range(REGIONS - 1)]
        result = [-0.25 * eps]
        for j in range(4):
            value = jnp.full((ROWS, LANES), taps[j][REGIONS - 1], jnp.float32)
            for r in range(REGIONS - 1):
                value = jnp.where(hits[r], taps[j][r], value)
            result.append(1.0 - eps * value if j == 0 else eps * value)
        return result

    for load in loads[:4]:
        load.wait()

    for f in range(FIELDS):
        packed[f] = zero

    def prepare(z, carry):
        at_z = (lane >= 8 * z) & (lane < 8 * z + 8)
        for lt in range(2):
            consts[1, z, :, lane_tile(lt)] = ids[z, :, lane_tile(lt)].astype(jnp.float32)
        weight = [mask[z, :, lane_tile(lt)].astype(jnp.float32) for lt in range(2)]
        for f in range(FIELDS):
            if f < 3 * PORTS:
                p, c = f // 3, f % 3
                tiles = []
                for lt in range(2):
                    value = own_m[p, c, z, :, lane_tile(lt)] * weight[lt]
                    own_m[p, c, z, :, lane_tile(lt)] = value
                    tiles.append(value)
            else:
                tiles = [consts[f - 3 * PORTS, z, :, lane_tile(lt)] for lt in range(2)]
            edge = jnp.where(lane < 4, tiles[0], tiles[1])
            packed[f] = jnp.where(at_z, pltpu.roll(edge, lax.rem(8 * z + 4, LANES), 1), packed[f])
        return carry

    lax.fori_loop(0, NZ, prepare, 0)

    peers = 0
    for dx, dy in NEIGHBOURS:
        peers = peers + jnp.where(there(dx, dy), 1, 0)
    pl.semaphore_wait(barrier, peers)

    def remote(index, src, dst, dx, dy):
        return pltpu.make_async_remote_copy(
            src_ref=src, dst_ref=dst, send_sem=send_sem.at[index], recv_sem=recv_sem.at[index],
            device_id=(gx + dx, gy + dy), device_id_type=MESH,
        )

    def rows_of(dx):
        return pl.ds(4, 4) if dx > 0 else pl.ds(0, 4)

    def port_copy(p, dx):
        side = 0 if dx > 0 else 1
        return remote(
            16 + 2 * p + side, own_m.at[p, :, pl.ds(0, NZ), rows_of(dx), :],
            halo_m.at[p, :, pl.ds(0, NZ), rows_of(dx), :], dx, 0,
        )

    edge_copies = []
    for dx, dy in EDGE_ORDER:
        if dy == 0:
            src, dst = packed.at[:, rows_of(dx), :], recv_x.at[:, rows_of(dx), :]
        elif dx == 0:
            src, dst = packed, recv_y.at[0 if dy > 0 else 1]
        else:
            src = packed.at[:, rows_of(dx), :]
            dst = recv_c.at[0 if dy > 0 else 1, :, rows_of(dx), :]
        edge_copies.append((dx, dy, remote(len(edge_copies), src, dst, dx, dy)))
    for dx in (1, -1):
        rows = pl.ds(5, 3) if dx > 0 else pl.ds(0, 3)
        edge_copies.append((dx, 0, remote(
            len(edge_copies), consts.at[:, :, rows, :], halo_consts.at[:, :, rows, :], dx, 0)))

    for dx, dy, copy in edge_copies:
        @pl.when(there(dx, dy))
        def _(copy=copy):
            copy.start()

    def start_port(p):
        for dx in (1, -1):
            @pl.when(there(dx, 0))
            def _(dx=dx):
                port_copy(p, dx).start()

    def sent_port(p):
        for dx in (1, -1):
            @pl.when(there(dx, 0))
            def _(dx=dx):
                port_copy(p, dx).wait_send()

    start_port(0)

    def coef_rows(source, rt):
        def body(z, carry):
            for lt in range(2):
                values = make_coefs(source[0, z, :, lane_tile(lt)], source[1, z, :, lane_tile(lt)])
                for k in range(5):
                    coefs[k, z, rt, :, lane_tile(lt)] = values[k]
            return carry

        lax.fori_loop(0, NZ, body, 0)

    coef_rows(consts, OWN)
    for dx, dy, copy in edge_copies:
        @pl.when(there(-dx, -dy))
        def _(copy=copy):
            copy.wait_recv()
    sent_port(0)
    start_port(1)
    coef_rows(halo_consts, HALO)
    for rt, middle, sides in ((OWN, packed, recv_y), (HALO, recv_x, recv_c)):
        for side in (LEFT, RIGHT):
            def joined(f):
                if side == LEFT:
                    return jnp.where(left_cols, sides[0, f], middle[f])
                return jnp.where(left_cols, middle[f], sides[1, f])

            for f in range(FIELDS - 2):
                strip_m[side, rt, f] = joined(f)
            values = make_coefs(joined(FIELDS - 2), joined(FIELDS - 1))
            for k in range(5):
                strip_coefs[side, rt, k] = values[k]

    def up_row(values):
        rolled = [pltpu.roll(value, ROWS - 1, 0) for value in values]
        return [
            jnp.where(last_row, rolled[1 - rt], rolled[rt]) for rt in (OWN, HALO)
        ]

    def down_row(values):
        rolled = [pltpu.roll(value, 1, 0) for value in values]
        return [
            jnp.where(first_row, rolled[1 - rt], rolled[rt]) for rt in (OWN, HALO)
        ]

    def up_col(tiles, inserted):
        rolled = [pltpu.roll(tile, LANES - 1, 1) for tile in tiles]
        return [
            jnp.where(last_lane, rolled[1], rolled[0]),
            jnp.where(last_lane, inserted, rolled[1]),
        ]

    def up_col_first(tiles, inserted):
        return [
            pltpu.roll(jnp.where(first_lane, tiles[1], tiles[0]), LANES - 1, 1),
            pltpu.roll(jnp.where(first_lane, inserted, tiles[1]), LANES - 1, 1),
        ]

    def down_col(tiles, inserted):
        rolled = [pltpu.roll(tile, 1, 1) for tile in tiles]
        return [
            jnp.where(first_lane, inserted, rolled[0]),
            jnp.where(first_lane, rolled[0], rolled[1]),
        ]

    def down_col_last(tiles, inserted):
        return [
            pltpu.roll(jnp.where(last_lane, inserted, tiles[0]), 1, 1),
            pltpu.roll(jnp.where(last_lane, tiles[0], tiles[1]), 1, 1),
        ]

    both = (OWN, HALO)

    def strip_up_z(value):
        return jnp.where(last_z, 0.0, pltpu.roll(value, LANES - 8, 1))

    def strip_down_z(value):
        return jnp.where(first_z, 0.0, pltpu.roll(value, 8, 1))

    def strip_steps(p):
        amplitude = [waveform[p, plan[s]] for s in range(STEPS)]
        el = [
            [[strip_m[side, rt, 3 * p + c] * amplitude[0] for rt in both] for c in range(3)]
            for side in (LEFT, RIGHT)
        ]
        mags = [None, None]
        sects = [[], []]
        for s in range(STEPS):
            ex, ez = el[RIGHT][0], el[RIGHT][2]
            for rt in both:
                edge_e[p, s, rt] = jnp.where(group == 5, pltpu.roll(ex[rt], 1, 1), ez[rt])
            for side in (LEFT, RIGHT):
                if side == RIGHT and s == STEPS - 1:
                    continue
                ex, ey, ez = el[side]
                ey_up, ez_up = up_row(ey), up_row(ez)
                new = [[None, None] for _ in range(3)]
                for rt in both:
                    curls = (
                        (pltpu.roll(ez[rt], LANES - 1, 1) - ez[rt]) - (strip_up_z(ey[rt]) - ey[rt]),
                        (strip_up_z(ex[rt]) - ex[rt]) - (ez_up[rt] - ez[rt]),
                        (ey_up[rt] - ey[rt]) - (pltpu.roll(ex[rt], LANES - 1, 1) - ex[rt]),
                    )
                    for c in range(3):
                        value = curls[c] if s == 0 else mags[side][c][rt] + curls[c]
                        if c != 1 and side == LEFT:
                            value = jnp.where(keep_low_y, value, 0.0)
                        if c != 0 and rt == HALO:
                            value = jnp.where(keep_low_x, value, 0.0)
                        new[c][rt] = value
                mags[side] = new
                hx, hy, hz = new
                if side == LEFT:
                    for rt in both:
                        edge_h[p, s, rt] = jnp.where(group == 4, pltpu.roll(hz[rt], 1, 1), hx[rt])
                if s == STEPS - 1:
                    continue
                hy_down, hz_down = down_row(hy), down_row(hz)
                sect = [[None, None] for _ in range(3)]
                after = [[None, None] for _ in range(3)]
                for rt in both:
                    backs = (
                        (hz[rt] - pltpu.roll(hz[rt], 1, 1)) - (hy[rt] - strip_down_z(hy[rt])),
                        (hx[rt] - strip_down_z(hx[rt])) - (hz[rt] - hz_down[rt]),
                        (hy[rt] - hy_down[rt]) - (hx[rt] - pltpu.roll(hx[rt], 1, 1)),
                    )
                    for c in range(3):
                        value = el[side][c][rt] + strip_coefs[side, rt, 0] * backs[c]
                        sect[c][rt] = value
                        result = strip_coefs[side, rt, 1] * value
                        for j in range(1, s + 1):
                            result = result - strip_coefs[side, rt, 1 + j] * sects[side][s - j][c][rt]
                        after[c][rt] = result + strip_m[side, rt, 3 * p + c] * amplitude[s + 1]
                sects[side].append(sect)
                el[side] = after

    def cell_pass(p, s, amplitude):
        last = s == STEPS - 1
        elec_in, elec_out = elecs[s % 2], elecs[(s + 1) % 2]
        magn_in, magn_out = magns[(s + 1) % 2], magns[s % 2]
        sources = (own_m, halo_m)

        def read_elec(c, z):
            if s == 0:
                return [[sources[rt][p, c, z, :, lane_tile(lt)] * amplitude[0] for lt in range(2)] for rt in both]
            return [[elec_in[c, z, rt, :, lane_tile(lt)] for lt in range(2)] for rt in both]

        def one_plane(z, el, el_up, mag_down):
            ex, ey, ez = el
            ey_xn = [up_row([ey[rt][lt] for rt in both]) for lt in range(2)]
            ez_xn = [up_row([ez[rt][lt] for rt in both]) for lt in range(2)]
            mags = [[[None] * 2 for _ in both] for _ in range(3)]
            for rt in both:
                inserted = insert_e[p, s, rt, z]
                ex_yn = up_col_first(ex[rt], inserted)
                if not (last and rt == HALO):
                    ez_yn = up_col(ez[rt], inserted)
                for lt in range(2):
                    for c in range(3):
                        if last and rt == HALO and c == 0:
                            continue
                        if c == 0:
                            value = (ez_yn[lt] - ez[rt][lt]) - (el_up[1][rt][lt] - ey[rt][lt])
                        elif c == 1:
                            value = (el_up[0][rt][lt] - ex[rt][lt]) - (ez_xn[lt][rt] - ez[rt][lt])
                        else:
                            value = (ey_xn[lt][rt] - ey[rt][lt]) - (ex_yn[lt] - ex[rt][lt])
                        if s > 0:
                            value = magn_in[c, z, rt, :, lane_tile(lt)] + value
                        if rt == HALO and c != 0:
                            value = jnp.where(keep_low_x, value, 0.0)
                        if not last:
                            magn_out[c, z, rt, :, lane_tile(lt)] = value
                        elif rt == OWN:
                            out_h[p, c, z, :, lane_tile(lt)] = -0.5 * value
                        mags[c][rt][lt] = value
            hx, hy, hz = mags
            hy_xp = [down_row([hy[rt][lt] for rt in both]) for lt in range(2)]
            hz_xp = [down_row([hz[rt][lt] for rt in both]) for lt in range(2)]
            for rt in both:
                if last and rt == HALO:
                    continue
                inserted = insert_h[p, s, rt, z]
                hx_yp = down_col_last(hx[rt], inserted)
                hz_yp = down_col(hz[rt], inserted)
                for lt in range(2):
                    hx_zp, hy_zp = mag_down[0][rt][lt], mag_down[1][rt][lt]
                    backs = (
                        (hz[rt][lt] - hz_yp[lt]) - (hy[rt][lt] - hy_zp),
                        (hx[rt][lt] - hx_zp) - (hz[rt][lt] - hz_xp[lt][rt]),
                        (hy[rt][lt] - hy_xp[lt][rt]) - (hx[rt][lt] - hx_yp[lt]),
                    )
                    factors = [coefs[k, z, rt, :, lane_tile(lt)] for k in range(2 + s)]
                    for c in range(3):
                        value = el[c][rt][lt] + factors[0] * backs[c]
                        new = factors[1] * value
                        for j in range(1, s + 1):
                            new = new - factors[1 + j] * sects[s - j][c, z, rt, :, lane_tile(lt)]
                        if last:
                            out_e[p, c, z, :, lane_tile(lt)] = new
                            continue
                        new = new + sources[rt][p, c, z, :, lane_tile(lt)] * amplitude[s + 1]
                        sects[s][c, z, rt, :, lane_tile(lt)] = value
                        elec_out[c, z, rt, :, lane_tile(lt)] = new
            return mags

        nothing = (zero, zero)
        kept = (OWN,) if last else both

        def body(block, carry):
            mags = [[list(carry[c][rt]) if rt in kept else nothing for rt in both] for c in range(2)]
            first = block * UNROLL
            el = [read_elec(c, first) for c in range(3)]
            for offset in range(UNROLL):
                last_offset = offset == UNROLL - 1
                el_up = [read_elec(c, first + offset + 1) for c in range(2 if last_offset else 3)]
                mags = one_plane(first + offset, el, el_up, mags)
                el = el_up
            return tuple(tuple(tuple(mags[c][rt]) for rt in kept) for c in range(2))

        lax.fori_loop(0, NZ // UNROLL, body, ((nothing,) * len(kept),) * 2)

    def strips(block, carry):
        for offset in range(2):
            strip_steps(2 * block + offset)
        return carry

    def place(index, carry):
        p, s = index // STEPS, lax.rem(index, STEPS)
        for rt in both:
            value_e, value_h = edge_e[p, s, rt], edge_h[p, s, rt]
            for z in range(NZ):
                insert_e[p, s, rt, z] = pltpu.roll(value_e, (251 - 8 * z) % LANES, 1)
                insert_h[p, s, rt, z] = pltpu.roll(value_h, (252 - 8 * z) % LANES, 1)
        return carry

    lax.fori_loop(0, PORTS // 2, strips, 0)
    lax.fori_loop(0, PORTS * STEPS, place, 0)
    sent_port(1)
    start_port(2)

    def port_body(p, carry):
        amplitude = [waveform[p, plan[s]] for s in range(STEPS)]
        for dx in (1, -1):
            @pl.when(there(-dx, 0))
            def _(dx=dx):
                port_copy(p, dx).wait_recv()

        for s in range(STEPS):
            if s == 1:
                @pl.when(p == 0)
                def _():
                    sent_port(2)
                    start_port(3)

            cell_pass(p, s, amplitude)
        return carry

    lax.fori_loop(0, PORTS, port_body, 0)

    for dx, dy, copy in edge_copies:
        @pl.when(there(dx, dy))
        def _(copy=copy):
            copy.wait_send()
    sent_port(PORTS - 1)


def local(residual, eps_inv, region_ids, source_mask, pole_a, pole_b, pole_c, waveform, plan):
    hbm = pl.BlockSpec(memory_space=pl.ANY)
    vmem = pl.BlockSpec(memory_space=pltpu.VMEM)
    shape = (PORTS, 3, NZ, ROWS, COLS)
    f32 = jnp.float32
    return pl.pallas_call(
        kernel,
        out_shape=[jax.ShapeDtypeStruct(shape, f32)] * 2,
        in_specs=[hbm] * 9,
        out_specs=[vmem] * 2,
        scratch_shapes=[
            *[pltpu.SMEM((2, REGIONS), f32)] * 3,
            pltpu.SMEM((PORTS, waveform.shape[0]), f32),
            pltpu.SMEM((STEPS,), jnp.int32),
            *[pltpu.VMEM((PORTS, 3, NZ + 1, ROWS, COLS), f32)] * 2,
            pltpu.VMEM((NZ, ROWS, COLS), jnp.int32),
            pltpu.VMEM((NZ, ROWS, COLS), jnp.int32),
            pltpu.VMEM((2, NZ, ROWS, COLS), f32),
            pltpu.VMEM((2, NZ, ROWS, COLS), f32),
            pltpu.VMEM((FIELDS, ROWS, LANES), f32),
            pltpu.VMEM((FIELDS, ROWS, LANES), f32),
            pltpu.VMEM((2, FIELDS, ROWS, LANES), f32),
            pltpu.VMEM((2, FIELDS, ROWS, LANES), f32),
            *[pltpu.VMEM((3, NZ + 1, 2, ROWS, COLS), f32)] * 2,
            *[pltpu.VMEM((3, NZ, 2, ROWS, COLS), f32)] * 5,
            pltpu.VMEM((5, NZ, 2, ROWS, COLS), f32),
            pltpu.VMEM((2, 2, 3 * PORTS, ROWS, LANES), f32),
            pltpu.VMEM((2, 2, 5, ROWS, LANES), f32),
            *[pltpu.VMEM((PORTS, STEPS, 2, ROWS, LANES), f32)] * 2,
            *[pltpu.VMEM((PORTS, STEPS, 2, NZ, ROWS, LANES), f32)] * 2,
            pltpu.SemaphoreType.DMA((9,)),
            pltpu.SemaphoreType.DMA((16 + 2 * PORTS,)),
            pltpu.SemaphoreType.DMA((16 + 2 * PORTS,)),
        ],
        compiler_params=pltpu.CompilerParams(
            collective_id=0, has_side_effects=True, vmem_limit_bytes=40 << 20
        ),
        cost_estimate=pl.CostEstimate(flops=60000000, bytes_accessed=5242880, transcendentals=0),
    )(*[
        pltpu.with_memory_space_constraint(value, pltpu.HBM)
        for value in (
            residual, eps_inv, region_ids, source_mask, pole_a.T, pole_b.T, pole_c.T, waveform.T, plan
        )
    ])


def solution(mesh):
    cells = P(None, "gx", "gy")
    fields = P(None, None, None, "gx", "gy")
    return jax.shard_map(
        local,
        mesh=mesh,
        in_specs=(fields, cells, cells, cells, P(), P(), P(), P(), P()),
        out_specs=(fields, fields),
        check_vma=False,
    )
```

time: 51 us -> 33.7 us (0.66)
  the two profiles are of different devices: /device:TPU:231 before, /device:TPU:6 now
where the time goes in v2:
time: 33.7 us; the launch traced here: 33.6 us
  Pallas kernels  30.6 us (91%)
  local copies, waits for them, and re-layouts  2.29 us (7%)
  between operations  0.64 us (2%)
    pallas_call x1, Pallas kernels, local(): pl.pallas_call(kernel, out_shape=[jax.ShapeDtypeStruct(shape, f32)] * 2,...  30.6 us
    unnamed x2, local copies, waits for them, and re-layouts  2.29 us

profile of v2, /device:TPU:6, one launch (start us, length us, event | category | flops | bytes accessed | tf_op | source)
XLA Modules:
  0.0 33.6 jit_solution(3104285405509752190)
XLA Ops:
  0.6 30.6 %shard_map.104 = (f32[4,3,16,8,256]{4,3,2,1,0:T(8,128)S(1)}, f32[4,3,16,8,256]{4,3,2,1,0:T(8,128)S(1)}) custom-call(f32[4,3,16,8,256]{4,3,2,1,0:T(8,128)} %residual.1, f32[16,8,256]{2,1,0:T(8,128)} %eps_inv.1, s32[16,8,256]{2,1,0:T(8,128)} %region_ids.1, s32[16,8,256]{2,1,0:T(8,128)} %source_mask.1, f32[2,8]{1,0:T(2,128)} %bitcast.5, f32[2,8]{1,0:T(2,128)} %bitcast.6, ...), custom_call_target="tpu_custom_call" | custom-call | flops 60000000 | bytes 5242880 | tf_op jit(solution)/shard_map/pallas_call | solution.py:504
  31.3 1.1 %copy.13 = f32[4,3,16,8,256]{4,3,2,1,0:T(8,128)} copy(f32[4,3,16,8,256]{4,3,2,1,0:T(8,128)S(1)} %get-tuple-element.4) | data formatting | bytes 3145728
  32.4 1.1 %copy.14 = f32[4,3,16,8,256]{4,3,2,1,0:T(8,128)} copy(f32[4,3,16,8,256]{4,3,2,1,0:T(8,128)S(1)} %get-tuple-element.5) | data formatting | bytes 3145728

commit v3 on v2

--- a/solution.py
+++ b/solution.py
@@ -242,13 +242,17 @@
         lax.fori_loop(0, NZ, body, 0)
 
     coef_rows(consts, OWN)
-    for dx, dy, copy in edge_copies:
+    for dx, dy, copy in edge_copies[len(EDGE_ORDER):]:
+        @pl.when(there(-dx, -dy))
+        def _(copy=copy):
+            copy.wait_recv()
+    coef_rows(halo_consts, HALO)
+    for dx, dy, copy in edge_copies[:len(EDGE_ORDER)]:
         @pl.when(there(-dx, -dy))
         def _(copy=copy):
             copy.wait_recv()
     sent_port(0)
     start_port(1)
-    coef_rows(halo_consts, HALO)
     for rt, middle, sides in ((OWN, packed, recv_y), (HALO, recv_x, recv_c)):
         for side in (LEFT, RIGHT):
             def joined(f):
@@ -456,17 +460,18 @@
             strip_steps(2 * block + offset)
         return carry
 
-    def place(index, carry):
-        p, s = index // STEPS, lax.rem(index, STEPS)
-        for rt in both:
-            value_e, value_h = edge_e[p, s, rt], edge_h[p, s, rt]
-            for z in range(NZ):
-                insert_e[p, s, rt, z] = pltpu.roll(value_e, (251 - 8 * z) % LANES, 1)
-                insert_h[p, s, rt, z] = pltpu.roll(value_h, (252 - 8 * z) % LANES, 1)
+    def place(p, carry):
+        for s in range(STEPS):
+            for rt in both:
+                value_e, value_h = edge_e[p, s, rt], edge_h[p, s, rt]
+                for z in range(NZ):
+                    insert_e[p, s, rt, z] = pltpu.roll(value_e, (251 - 8 * z) % LANES, 1)
+                    if rt == OWN or s < STEPS - 1:
+                        insert_h[p, s, rt, z] = pltpu.roll(value_h, (252 - 8 * z) % LANES, 1)
         return carry
 
     lax.fori_loop(0, PORTS // 2, strips, 0)
-    lax.fori_loop(0, PORTS * STEPS, place, 0)
+    lax.fori_loop(0, PORTS, place, 0)
     sent_port(1)
     start_port(2)
 

time: 33.7 us -> 33.1 us (0.982)
  Pallas kernels: 30.6 us -> 30.1 us
    pallas_call x1, Pallas kernels: 30.6 us -> 30.1 us  [local(): pl.pallas_call(kernel, out_shape=[jax.ShapeDtypeStruct(shape, f32)] * 2,...]
where the time goes in v3:
time: 33.1 us; the launch traced here: 33 us
  Pallas kernels  30.1 us (91%)
  local copies, waits for them, and re-layouts  2.29 us (7%)
  between operations  0.64 us (2%)
    pallas_call x1, Pallas kernels, local(): pl.pallas_call(kernel, out_shape=[jax.ShapeDtypeStruct(shape, f32)] * 2,...  30.1 us
    unnamed x2, local copies, waits for them, and re-layouts  2.29 us

profile of v3, /device:TPU:6, one launch (start us, length us, event | category | flops | bytes accessed | tf_op | source)
XLA Modules:
  0.0 33.0 jit_solution(14723323714292737694)
XLA Ops:
  0.6 30.1 %shard_map.104 = (f32[4,3,16,8,256]{4,3,2,1,0:T(8,128)S(1)}, f32[4,3,16,8,256]{4,3,2,1,0:T(8,128)S(1)}) custom-call(f32[4,3,16,8,256]{4,3,2,1,0:T(8,128)} %residual.1, f32[16,8,256]{2,1,0:T(8,128)} %eps_inv.1, s32[16,8,256]{2,1,0:T(8,128)} %region_ids.1, s32[16,8,256]{2,1,0:T(8,128)} %source_mask.1, f32[2,8]{1,0:T(2,128)} %bitcast.5, f32[2,8]{1,0:T(2,128)} %bitcast.6, ...), custom_call_target="tpu_custom_call" | custom-call | flops 60000000 | bytes 5242880 | tf_op jit(solution)/shard_map/pallas_call | solution.py:509
  30.7 1.1 %copy.13 = f32[4,3,16,8,256]{4,3,2,1,0:T(8,128)} copy(f32[4,3,16,8,256]{4,3,2,1,0:T(8,128)S(1)} %get-tuple-element.4) | data formatting | bytes 3145728
  31.9 1.1 %copy.14 = f32[4,3,16,8,256]{4,3,2,1,0:T(8,128)} copy(f32[4,3,16,8,256]{4,3,2,1,0:T(8,128)S(1)} %get-tuple-element.5) | data formatting | bytes 3145728
